TPU v7x, 512 devices: a whole 4x8x8 slice. The times are simulated.
512 devices in a mesh: date: 64 (over z, x, core), space: 8 (over y).
Axes of the slice: x: 4, y: 8, z: 8, core: 2. Of those that a mesh axis runs over, the one named last changes fastest.
Arguments:
- chips: bfloat16 [1024, 8, 4096], P('date', 'space'), may hold values from -150 to 150
- pair_target: int32 [4096, 1], P('date'), may hold values from 0 to 63; in each aligned block of 64 rows (0 to 63, 64 to 127, ...) at most 2 rows name the same one
- pair_slot: int32 [4096], P('date'), may hold values from 0 to 15
- offset_fix: int32 [4096, 8, 2], P('date', 'space'), may hold values from -192 to 192
Outputs:
- displacement: float32 [2, 1024, 8], P(None, 'date', 'space')
- pair_measure: float32 [3, 4096, 8], P(None, 'date', 'space')
Inputs may be any that keep to these rules, and one draw needn't show every extreme that they name: `pair_target`: in the 64 rows of one index of date, no value is named more than 2 times, and in some of those blocks a value is named exactly 2 times.
All inputs are finite; a program needn't handle non-finite values.
Results may differ from a plain program's by a relative error of at most 0.0015.
Values may be sent and summed in bfloat16 or wider, within the bound.
A program may use at most 64 MiB of HBM per device.

v0:
```python
import jax
import jax.numpy as jnp
from jax import lax
from jax.sharding import PartitionSpec as P

CHIP = 64
LINKS = 4


SIGMA = 0.6
STEP = 1.0
ZSCALE = 0.5
EPS = 1e-06
LAMBDA = 2.0
MUS = (4.0, 2.0, 1.0)
FIXED = 32.0


def padded_2(cells, sides, width):
    for axis, dim in sides:
        count = lax.axis_size(axis)
        ends = count - 1
        head = lax.slice_in_dim(cells, 0, width, axis=dim)
        tail = lax.slice_in_dim(cells, cells.shape[dim] - width, cells.shape[dim], axis=dim)
        cells = jnp.concatenate(
            [
                lax.ppermute(tail, axis, [(i, (i + 1) % count) for i in range(ends)]),
                cells,
                lax.ppermute(head, axis, [((i + 1) % count, i) for i in range(ends)]),
            ],
            axis=dim,
        )
    return cells


def kernels(shifts):
    positions = jnp.arange(CHIP, dtype=jnp.float32)
    spacing = positions[:, None] - positions[None, :]
    distance = spacing - shifts[..., None, None]
    return jnp.exp(-(distance * distance) / (2.0 * SIGMA * SIGMA)).astype(jnp.bfloat16)


def correlate_rows(first, second, offsets):
    levels = STEP * (jnp.arange(3, dtype=jnp.float32) - 1.0)
    shifts = offsets[:, :, None] + levels
    kernel_y = kernels(shifts[:, 0])
    kernel_x = kernels(shifts[:, 1])
    first_mat = first.reshape(-1, CHIP, CHIP)
    second_mat = second.reshape(-1, CHIP, CHIP)
    moved = jnp.einsum(
        "qak,qxnk->qxan", first_mat, kernel_x, preferred_element_type=jnp.float32
    ).astype(jnp.bfloat16)
    lifted = jnp.einsum(
        "qymk,qmn->qykn", kernel_y, second_mat, preferred_element_type=jnp.float32
    ).astype(jnp.bfloat16)
    inner = jnp.einsum("qykn,qxkn->qyx", lifted, moved, preferred_element_type=jnp.float32)
    first_norm = jnp.einsum("qa,qa->q", first, first, preferred_element_type=jnp.float32)
    second_norm = jnp.einsum("qa,qa->q", second, second, preferred_element_type=jnp.float32)
    scores = CHIP * inner / jnp.sqrt((first_norm + EPS) * (second_norm + EPS))[:, None, None]
    raised = jnp.exp(ZSCALE * scores)
    weights = raised / jnp.sum(raised, axis=(1, 2), keepdims=True)
    move_y = offsets[:, 0] + jnp.sum(jnp.sum(weights, axis=2) * levels, axis=1)
    move_x = offsets[:, 1] + jnp.sum(jnp.sum(weights, axis=1) * levels, axis=1)
    quality = jax.nn.sigmoid(ZSCALE * jnp.sum(weights * scores, axis=(1, 2)))
    return jnp.stack([move_y, move_x, quality], axis=1)


def make_correlator(chips):

    def correlate_received(received):
        recv_chips, recv_meta, recv_offset = received
        sources = recv_meta.shape[0]
        items = recv_meta.shape[1]
        chip_dev = recv_chips.shape[2]
        partner = jnp.maximum(recv_meta[:, :, 0], 0)
        own_chips = chips[partner]
        groups = sources // 8
        first_rows = recv_chips.reshape(groups, -1, CHIP * CHIP)
        second_rows = own_chips.reshape(groups, -1, CHIP * CHIP)
        offset_rows = (recv_offset.astype(jnp.float32) / FIXED).reshape(groups, -1, 2)

        def group_measure(packed):
            return correlate_rows(packed[0], packed[1], packed[2])

        result = lax.map(group_measure, (first_rows, second_rows, offset_rows))
        result = result.reshape(sources, items, chip_dev, 3)
        validity = (recv_meta[:, :, 0] >= 0).astype(jnp.float32)
        quality = result[:, :, :, 2] * validity[:, :, None]
        measured = jnp.concatenate([result[:, :, :, :2], quality[:, :, :, None]], axis=3)
        return (jnp.transpose(measured, (0, 1, 3, 2)), recv_meta)

    return correlate_received


def slot_layout(pair_target, date_count):
    pair_dev = pair_target.shape[0]
    capacity = 2 * pair_dev // date_count
    target = pair_target[:, 0]
    onehot = (target[:, None] == jnp.arange(date_count, dtype=jnp.int32)[None, :]).astype(
        jnp.float32
    )
    lower = (jnp.arange(pair_dev)[:, None] > jnp.arange(pair_dev)[None, :]).astype(jnp.float32)
    before = jnp.dot(lower, onehot, precision=lax.Precision.HIGHEST)
    ranking = jnp.sum(before * onehot, axis=1).astype(jnp.int32)
    return (target * capacity + ranking, capacity)


def per_device(chips, pair_target, pair_slot, offset_fix):
    date_dev, chip_dev, area = chips.shape
    date_count = lax.axis_size("date")
    pair_dev = pair_target.shape[0]
    slot_index, capacity = slot_layout(pair_target, date_count)
    slot_total = date_count * capacity
    position = lax.axis_index("date")
    first_local = jnp.arange(pair_dev, dtype=jnp.int32) // LINKS
    first_global = position * date_dev + first_local
    send_chips = (
        jnp.zeros((slot_total, chip_dev, area), jnp.bfloat16).at[slot_index].set(chips[first_local])
    )
    send_meta = (
        jnp.full((slot_total, 2), -1, jnp.int32)
        .at[slot_index]
        .set(jnp.stack([pair_slot, first_global], axis=1))
    )
    send_offset = jnp.zeros((slot_total, chip_dev, 2), jnp.int32).at[slot_index].set(offset_fix)
    send_chips = send_chips.reshape(date_count, capacity, chip_dev, area)
    send_meta = send_meta.reshape(date_count, capacity, 2)
    send_offset = send_offset.reshape(date_count, capacity, chip_dev, 2)
    correlator = make_correlator(chips)
    received = (
        lax.all_to_all(send_chips, "date", split_axis=0, concat_axis=0, tiled=True),
        lax.all_to_all(send_meta, "date", split_axis=0, concat_axis=0, tiled=True),
        lax.all_to_all(send_offset, "date", split_axis=0, concat_axis=0, tiled=True),
    )
    measured, recv_meta = correlator(received)
    returned_measure = lax.all_to_all(measured, "date", split_axis=0, concat_axis=0, tiled=True)
    picked_measure = returned_measure.reshape(slot_total, 3, chip_dev)[slot_index]
    measured = measured.reshape(slot_total, 3, chip_dev)
    meta_flat = recv_meta.reshape(slot_total, 2)
    measure = measured[:, :2, :]
    quality = measured[:, 2, :]
    second_local = jnp.maximum(meta_flat[:, 0], 0)
    first_index = jnp.maximum(meta_flat[:, 1], 0)
    to_local = (meta_flat[:, 0][:, None] == jnp.arange(date_dev, dtype=jnp.int32)[None, :]).astype(
        jnp.float32
    )
    all_dates = jnp.arange(date_dev * date_count, dtype=jnp.int32)
    to_global = (first_index[:, None] == all_dates[None, :]).astype(jnp.float32)
    field = jnp.zeros((date_dev, 2, chip_dev), jnp.float32)
    for scale in MUS:
        everyone = lax.all_gather(field, "date", axis=0, tiled=True)
        first_val = everyone[first_index]
        second_val = field[second_local]
        resid = measure - (second_val - first_val)
        spread = scale * scale
        weight = quality * spread / (spread + jnp.sum(resid * resid, axis=1))
        to_second = jnp.concatenate(
            [weight[:, None] * (first_val + measure), weight[:, None]], axis=1
        )
        to_first = jnp.concatenate(
            [weight[:, None] * (second_val - measure), weight[:, None]], axis=1
        )
        local_sum = jnp.einsum("sd,scn->dcn", to_local, to_second, precision=lax.Precision.HIGHEST)
        remote_sum = lax.psum_scatter(
            jnp.einsum("sd,scn->dcn", to_global, to_first, precision=lax.Precision.HIGHEST),
            "date",
            scatter_dimension=0,
            tiled=True,
        )
        totals = local_sum + remote_sum
        padded = padded_2(field, (("space", 2),), 1)
        beside = padded[:, :, :-2] + padded[:, :, 2:]
        field = (LAMBDA * beside + totals[:, :2]) / (2.0 * LAMBDA + totals[:, 2:3])
    return (jnp.transpose(field, (1, 0, 2)), jnp.transpose(picked_measure, (1, 0, 2)))


def solution(mesh):
    in_specs = (P("date", "space", None), P("date", None), P("date"), P("date", "space", None))
    out_specs = (P(None, "date", "space"), P(None, "date", "space"))
    return jax.shard_map(
        per_device, mesh=mesh, in_specs=in_specs, out_specs=out_specs, check_vma=False
    )
```

profile of v0, /device:TPU:1, one launch (start us, length us, event | category | flops | bytes accessed | tf_op | source)
XLA Modules:
  0.0 993.9 jit_solution(11289454173240843894)
XLA Ops:
  4.8 14.8 %all-to-all-start = ((s32[64,2,2]{1,2,0:T(2,128)}), s32[64,2,2]{1,2,0:T(2,128)S(1)}, u32[]{:S(2)}, u32[]{:S(2)}) async-start(s32[64,2,2]{1,2,0:T(2,128)} %copy.266), calls=%async_computation | async-start | bytes 131072 | tf_op jit(solution)/shard_map/all_to_all | solution.py:132
  22.3 7.4 all-to-all-done
  29.8 4.4 all-to-all-start.1
  34.2 3.2 scatter_custom_fusion.2
  38.9 5.4 all-to-all-done.1
  44.3 5.0 all-to-all-start.2
  49.4 3.2 collective-permute-start
  59.5 17.8 %all-to-all-done.2 = bf16[64,2,1,4096]{3,1,2,0:T(2,128)(2,1)S(1)} async-done(((bf16[64,2,1,4096]{3,1,2,0:T(2,128)(2,1)}), bf16[64,2,1,4096]{3,1,2,0:T(2,128)(2,1)S(1)}, u32[]{:S(2)}, u32[]{:S(2)}) %all-to-all-start.2) | async-done | bytes 1048608 | tf_op jit(solution)/shard_map/all_to_all | solution.py:131
  78.6 50.1 %while.12 = (s32[]{:T(128)}, f32[8,16,3]{1,0,2:T(8,128)S(1)}, f32[8,16,2]{1,0,2:T(8,128)S(1)}, bf16[8,16,4096]{2,1,0:T(8,128)(2,1)S(1)}, bf16[8,16,4096]{2,1,0:T(8,128)(2,1)}, /*index=5*/s32[]{:T(128)}, s32[]{:T(128)}) while((s32[]{:T(128)}, f32[8,16,3]{1,0,2:T(8,128)S(1)}, f32[8,16,2]{1,0,2:T(8,128)S(1)}, ...), condition=%wide.region_11.12_spmd, body=%wide.region_4.11_spmd.sunk | while | flops 54269684 | bytes 3727045 | solution.py:85
  82.4 1.8 fusion.70
  88.6 1.8 fusion.70
  94.9 1.8 fusion.70
  101.2 1.8 fusion.70
  107.4 1.8 fusion.70
  113.7 1.8 fusion.70
  120.0 1.8 fusion.70
  130.9 242.9 %all-reduce = f32[1024,3,1]{0,1,2:T(4,128)S(1)} all-reduce(f32[1024,3,1]{0,1,2:T(4,128)S(1)} %convolution_bitcast_fusion.3), channel_id=2, replica_groups=mesh['date'=64,'space'=8] {'date'}, use_global_device_ids=true, to_apply=%region_13.14.clone | all-reduce | flops 3072 | bytes 24576
  374.8 52.5 %all_gather.7 = f32[1024,2,1]{1,2,0:T(1,128)S(1)} all-gather(f32[16,2,1]{1,2,0:T(1,128)S(1)} %copy.290), channel_id=1, replica_groups=mesh['date'=64,'space'=8] {'date'}, dimensions={0}, use_global_device_ids=true | all-gather | bytes 8320 | tf_op jit(solution)/shard_map/all_gather | solution.py:151
  428.5 3.2 collective-permute-start.2
  433.6 243.2 %all-reduce.1 = f32[1024,3,1]{0,1,2:T(4,128)S(1)} all-reduce(f32[1024,3,1]{0,1,2:T(4,128)S(1)} %convolution_bitcast_fusion.2), channel_id=3, replica_groups=mesh['date'=64,'space'=8] {'date'}, use_global_device_ids=true, to_apply=%region_15.16.clone | all-reduce | flops 3072 | bytes 24576
  677.8 11.5 %all-to-all-start.3 = ((f32[64,2,3,1]{2,1,3,0:T(2,128)}), f32[64,2,3,1]{2,1,3,0:T(2,128)S(1)}, u32[]{:S(2)}, u32[]{:S(2)}) async-start(f32[64,2,3,1]{2,1,3,0:T(2,128)} %copy.310), calls=%async_computation.3 | async-start | bytes 131072 | tf_op jit(solution)/shard_map/all_to_all | solution.py:136
  690.2 51.4 %all_gather.8 = f32[1024,2,1]{1,2,0:T(1,128)S(1)} all-gather(f32[16,2,1]{1,2,0:T(1,128)S(1)} %copy.300), channel_id=1, replica_groups=mesh['date'=64,'space'=8] {'date'}, dimensions={0}, use_global_device_ids=true | all-gather | bytes 8320 | tf_op jit(solution)/shard_map/all_gather | solution.py:151
  742.7 4.0 collective-permute-start.4
  748.6 243.2 %all-reduce.2 = f32[1024,3,1]{0,1,2:T(4,128)S(1)} all-reduce(f32[1024,3,1]{0,1,2:T(4,128)S(1)} %convolution_bitcast_fusion.1), channel_id=4, replica_groups=mesh['date'=64,'space'=8] {'date'}, use_global_device_ids=true, to_apply=%region_17.18.clone | all-reduce | flops 3072 | bytes 24576
  (307 shorter events, 65.8 us)
Async XLA Ops:
  0.6 33.6 %copy-start = (bf16[16,1,4096]{2,0,1:T(8,128)(2,1)S(1)}, bf16[16,1,4096]{2,0,1:T(8,128)(2,1)}, u32[]{:S(2)}) copy-start(bf16[16,1,4096]{2,0,1:T(8,128)(2,1)} %param.6) | copy-start | bytes 393220
  4.8 24.9 %all-to-all-start = ((s32[64,2,2]{1,2,0:T(2,128)}), s32[64,2,2]{1,2,0:T(2,128)S(1)}, u32[]{:S(2)}, u32[]{:S(2)}) async-start(s32[64,2,2]{1,2,0:T(2,128)} %copy.266), calls=%async_computation | async-start | bytes 131072 | tf_op jit(solution)/shard_map/all_to_all | solution.py:132
  29.8 14.6 %all-to-all-start.1 = ((s32[64,2,1,2]{1,3,2,0:T(2,128)}), s32[64,2,1,2]{1,3,2,0:T(2,128)S(1)}, u32[]{:S(2)}, u32[]{:S(2)}) async-start(s32[64,2,1,2]{1,3,2,0:T(2,128)} %copy.270), calls=%async_computation.1 | async-start | bytes 131072 | tf_op jit(solution)/shard_map/all_to_all | solution.py:133
  44.3 33.0 %all-to-all-start.2 = ((bf16[64,2,1,4096]{3,1,2,0:T(2,128)(2,1)}), bf16[64,2,1,4096]{3,1,2,0:T(2,128)(2,1)S(1)}, u32[]{:S(2)}, u32[]{:S(2)}) async-start(bf16[64,2,1,4096]{3,1,2,0:T(2,128)(2,1)} %reshape.562), calls=%async_computation.2 | async-start | bytes 2097152 | tf_op jit(solution)/shard_map/all_to_all | solution.py:131
  49.4 324.6 %collective-permute-start = (f32[16,2,1]{0,1,2:T(2,128)S(1)}, f32[16,2,1]{0,1,2:T(2,128)S(1)}, u32[]{:S(2)}, u32[]{:S(2)}) collective-permute-start(f32[16,2,1]{0,1,2:T(2,128)S(1)} %broadcast_in_dim.20), channel_id=1, source_target_pairs={{0,1},{1,2},{2,3},{3,4},{4,5},{5,6},{6,7},{8,9},{9,10},{10,11},{11... | collective-permute-start | bytes 392 | tf_op jit(solution)/shard_map/ppermute | solution.py:27
  52.6 321.4 %collective-permute-start.1 = (f32[16,2,1]{0,1,2:T(2,128)S(1)}, f32[16,2,1]{0,1,2:T(2,128)S(1)}, u32[]{:S(2)}, u32[]{:S(2)}) collective-permute-start(f32[16,2,1]{0,1,2:T(2,128)S(1)} %broadcast_in_dim.20), channel_id=1, source_target_pairs={{1,0},{2,1},{3,2},{4,3},{5,4},{6,5},{7,6},{9,8},{10,9},{11,10},{12... | collective-permute-start | bytes 392 | tf_op jit(solution)/shard_map/ppermute | solution.py:29
  428.5 260.8 %collective-permute-start.2 = (f32[16,2,1]{0,1,2:T(2,128)S(1)}, f32[16,2,1]{0,1,2:T(2,128)S(1)}, u32[]{:S(2)}, u32[]{:S(2)}) collective-permute-start(f32[16,2,1]{0,1,2:T(2,128)S(1)} %add_divide_fusion.2), channel_id=1, source_target_pairs={{0,1},{1,2},{2,3},{3,4},{4,5},{5,6},{6,7},{8,9},{9,10},{10,11},{11... | collective-permute-start | bytes 392 | tf_op jit(solution)/shard_map/ppermute | solution.py:27
  431.7 257.6 %collective-permute-start.3 = (f32[16,2,1]{0,1,2:T(2,128)S(1)}, f32[16,2,1]{0,1,2:T(2,128)S(1)}, u32[]{:S(2)}, u32[]{:S(2)}) collective-permute-start(f32[16,2,1]{0,1,2:T(2,128)S(1)} %add_divide_fusion.2), channel_id=1, source_target_pairs={{1,0},{2,1},{3,2},{4,3},{5,4},{6,5},{7,6},{9,8},{10,9},{11,10},{12... | collective-permute-start | bytes 392 | tf_op jit(solution)/shard_map/ppermute | solution.py:29
  677.8 314.8 %all-to-all-start.3 = ((f32[64,2,3,1]{2,1,3,0:T(2,128)}), f32[64,2,3,1]{2,1,3,0:T(2,128)S(1)}, u32[]{:S(2)}, u32[]{:S(2)}) async-start(f32[64,2,3,1]{2,1,3,0:T(2,128)} %copy.310), calls=%async_computation.3 | async-start | bytes 131072 | tf_op jit(solution)/shard_map/all_to_all | solution.py:136
  742.7 249.4 %collective-permute-start.4 = (f32[16,2,1]{0,1,2:T(2,128)S(1)}, f32[16,2,1]{0,1,2:T(2,128)S(1)}, u32[]{:S(2)}, u32[]{:S(2)}) collective-permute-start(f32[16,2,1]{0,1,2:T(2,128)S(1)} %add_divide_fusion.1), channel_id=1, source_target_pairs={{0,1},{1,2},{2,3},{3,4},{4,5},{5,6},{6,7},{8,9},{9,10},{10,11},{11... | collective-permute-start | bytes 392 | tf_op jit(solution)/shard_map/ppermute | solution.py:27
  746.7 245.4 %collective-permute-start.5 = (f32[16,2,1]{0,1,2:T(2,128)S(1)}, f32[16,2,1]{0,1,2:T(2,128)S(1)}, u32[]{:S(2)}, u32[]{:S(2)}) collective-permute-start(f32[16,2,1]{0,1,2:T(2,128)S(1)} %add_divide_fusion.1), channel_id=1, source_target_pairs={{1,0},{2,1},{3,2},{4,3},{5,4},{6,5},{7,6},{9,8},{10,9},{11,10},{12... | collective-permute-start | bytes 392 | tf_op jit(solution)/shard_map/ppermute | solution.py:29
where the time goes:
time: 1000 us; the launch traced here: 994 us
  blocking collectives  833 us (83%)
  starting transfers between devices  50.2 us (5%)
  local copies, waits for them, and re-layouts  35.5 us (4%)
  waiting for transfers between devices  30.7 us (3%)
  matrix products  26.3 us (3%)
  other arithmetic  15.4 us (2%)
    unnamed x3, blocking collectives  729 us
    all_gather x2, blocking collectives, per_device(): everyone = lax.all_gather(field, 'date', axis=0, tiled=True)  104 us
  transfers between devices with their start and end apart: 10, of which 3 were waited for; matrix products, arithmetic and copies ran while one was open for 7% of the time, Pallas kernels for 0%

commit v1 on v0

v1 whole, which is shorter than its diff:
```python
import jax
import jax.numpy as jnp
from jax import lax
from jax.experimental import pallas as pl
from jax.experimental.pallas import tpu as pltpu
from jax.sharding import PartitionSpec as P

CHIP = 64
LINKS = 4
ROW = 8
NZ = 8
DATE_DEV = 16
PAIRS = 64
HALF = 8
SIGMA = 0.6
ZSCALE = 0.5
EPS = 1e-06
LAMBDA = 2.0
MUS = (4.0, 2.0, 1.0)
FIXED = 32.0
ITEMS = 11
F32 = jnp.float32
BF16 = jnp.bfloat16
PRE = (16, 16, 16, 16)


def iota(shape, dim):
    return lax.broadcasted_iota(jnp.int32, shape, dim)


def fold(rows):
    return jnp.sum(rows.reshape(rows.shape[0] // 8, 8, 128), axis=0)


def split_bf16(value):
    high = value.astype(BF16)
    return high, (value - high.astype(F32)).astype(BF16)


def kernel(
    chips,
    target,
    slot,
    offs_s,
    offs_v,
    measure_out,
    disp_out,
    tmp,
    held0,
    held1,
    held2,
    held3,
    held4,
    held5,
    held6,
    held7,
    xsend,
    recv,
    bnorm,
    rowx,
    zsec,
    reqv,
    req,
    mbuf,
    lhs,
    onehot,
    member,
    sums,
    mrow,
    mall,
    spread,
    fsend,
    halo,
    sem_req,
    row_s,
    row_r,
    zsec_s,
    zsec_r,
    plus_s,
    plus_r,
    minus_s,
    minus_r,
    x_s,
    x_r,
    mrow_s,
    mrow_r,
    mall_s,
    mall_r,
    halo_s,
    halo_r,
):
    held = (held0, held1, held2, held3, held4, held5, held6, held7)
    date = lax.axis_index("date")
    y = lax.axis_index("space")
    ny = lax.axis_size("space")
    mz = lax.div(date, ROW)
    me = lax.rem(date, ROW)

    def row_peer(k):
        return {"date": mz * ROW + lax.rem(me + k, ROW)}

    def z_peer(k):
        return {"date": lax.rem(mz + k, NZ) * ROW + me}

    def y_peer(k):
        return {"space": lax.rem(y + k, ny)}

    def remote(src, dst, ssem, rsem, peer):
        return pltpu.make_async_remote_copy(
            src_ref=src,
            dst_ref=dst,
            send_sem=ssem,
            recv_sem=rsem,
            device_id=peer,
            device_id_type=pl.DeviceIdType.MESH,
        )

    barrier = pltpu.get_barrier_semaphore()
    for k in range(1, ROW):
        pl.semaphore_signal(barrier, inc=1, device_id=row_peer(k), device_id_type=pl.DeviceIdType.MESH)
    for k in range(1, NZ):
        pl.semaphore_signal(barrier, inc=1, device_id=z_peer(k), device_id_type=pl.DeviceIdType.MESH)
    for k in (1, ny - 1):
        pl.semaphore_signal(barrier, inc=1, device_id=y_peer(k), device_id_type=pl.DeviceIdType.MESH)

    for j in range(32):
        tmp[pl.ds(j, DATE_DEV, stride=32), :] = chips[:, 128 * j : 128 * j + 128].astype(F32)
    for d in range(DATE_DEV):
        own = tmp[pl.ds(32 * d, 32), :]
        held[0][d] = own.astype(BF16)
        bnorm[pl.ds(8 * d, 8), :] = fold(own * own)

    sub = iota((PAIRS, 128), 0)
    lane = iota((PAIRS, 128), 1)
    zeros64 = jnp.zeros((1, 128 - PAIRS), jnp.int32)
    trow = jnp.concatenate([target[...], zeros64 - 1], axis=1).astype(F32)
    srow = jnp.concatenate([slot[...], zeros64], axis=1).astype(F32)
    tb = jnp.broadcast_to(trow, (PAIRS, 128))
    sb = jnp.broadcast_to(srow, (PAIRS, 128))
    eye = sub == lane
    tcol = jnp.sum(jnp.where(eye, tb, 0.0), axis=1, keepdims=True)
    scol = jnp.sum(jnp.where(eye, sb, 0.0), axis=1, keepdims=True)
    twin = jnp.where((tcol == tb) & (lane < sub), 1.0, 0.0)
    place = 2.0 * tcol + jnp.sum(twin, axis=1, keepdims=True)
    wanted = jnp.sum(jnp.where(lane.astype(F32) == place, scol, 0.0), axis=0, keepdims=True)
    place_row = jnp.sum(jnp.where(eye, place, 0.0), axis=0, keepdims=True)
    deal = jnp.where(lane == me * DATE_DEV + sub // LINKS, 1.0, 0.0).astype(BF16)
    r8 = iota((8, PAIRS), 0)
    l8 = iota((8, PAIRS), 1)
    ours = (l8 % LINKS) == (r8 % LINKS)
    named = jnp.where(r8 < 4, jnp.broadcast_to(trow[:, :PAIRS], (8, PAIRS)), jnp.broadcast_to(srow[:, :PAIRS], (8, PAIRS)))
    named = jnp.where(ours, named, 0.0).astype(BF16)
    rowx[pl.ds(0, 8), :] = jnp.dot(named, deal, preferred_element_type=F32)
    rowx[pl.ds(8, 8), :] = jnp.broadcast_to(wanted, (8, 128))

    pl.semaphore_wait(barrier, ROW - 1 + NZ - 1 + 2)

    def row_copy(k):
        return remote(rowx.at[pl.ds(0, 16)], rowx.at[pl.ds(16 * k, 16)], row_s.at[k], row_r.at[k], row_peer(k))

    def ring_part(t, half):
        return held[t].at[pl.ds(half * HALF, HALF)]

    def plus_copy(s, half):
        return remote(
            ring_part(max(2 * s - 3, 0), half),
            ring_part(2 * s - 1, half),
            plus_s.at[s - 1, half],
            plus_r.at[s - 1, half],
            z_peer(1),
        )

    def minus_copy(s, half):
        return remote(
            ring_part(2 * s - 2, half),
            ring_part(min(2 * s, 7), half),
            minus_s.at[s - 1, half],
            minus_r.at[s - 1, half],
            z_peer(NZ - 1),
        )

    def plus_arrived(s, half):
        plus_copy(s, half).wait_recv()

    def minus_arrived(s, half):
        minus_copy(s, half).wait_recv()

    for k in range(1, ROW):
        row_copy(k).start()
    for half in (0, 1):
        plus_copy(1, half).start()
        minus_copy(1, half).start()
    for k in range(1, ROW):
        row_copy(k).wait_recv()

    reqv[pl.ds(0, 8), :] = rowx[pl.ds(8, 8, stride=16), :].astype(jnp.int32)
    reqv[pl.ds(8, 8), :] = jnp.broadcast_to(place_row, (8, 128)).astype(jnp.int32)
    fetch = pltpu.make_async_copy(reqv, req, sem_req)
    fetch.start()
    total = rowx[pl.ds(0, 8), :]
    for k in range(1, ROW):
        total = total + rowx[pl.ds(16 * k, 8), :]
    zsec[pl.ds(8 * mz, 8), :] = total

    def zsec_copy(k):
        mine = zsec.at[pl.ds(8 * mz, 8)]
        return remote(mine, mine, zsec_s.at[k], zsec_r.at[k], z_peer(k))

    def zsec_arrived(k):
        theirs = zsec.at[pl.ds(8 * lax.rem(mz - k + NZ, NZ), 8)]
        remote(theirs, theirs, zsec_s.at[k], zsec_r.at[k], z_peer(k)).wait_recv()

    for k in range(1, NZ):
        zsec_copy(k).start()
    fetch.wait()

    def x_copy(t, k, block):
        return remote(
            xsend.at[pl.ds((t * ROW + k) * 2, 2)],
            recv.at[pl.ds(block * 16 + me * 2, 2)],
            x_s.at[t, k],
            x_r.at[t, k],
            row_peer(k),
        )

    def x_arrived(t, k, block):
        theirs = recv.at[pl.ds(block * 16 + lax.rem(me - k + ROW, ROW) * 2, 2)]
        remote(xsend.at[pl.ds((t * ROW + k) * 2, 2)], theirs, x_s.at[t, k], x_r.at[t, k], row_peer(k)).wait_recv()

    def block_of(t):
        step = (t + 1) // 2
        return lax.rem(mz - step + NZ, NZ) if t % 2 else lax.rem(mz + step, NZ)

    def serve(t):
        block = block_of(t)
        for k in (1, 7, 2, 6, 3, 5, 4, 0):
            asker = (ROW - k) % ROW
            for r in (0, 1):
                chip = held[t][jnp.clip(req[asker, block * 16 + me * 2 + r], 0, DATE_DEV - 1)]
                if k:
                    xsend[(t * ROW + k) * 2 + r] = chip
                else:
                    recv[block * 16 + me * 2 + r] = chip
            if k:
                x_copy(t, k, block).start()

    lane64 = iota((CHIP, 128), 1)
    spacing_x = ((lane64 % CHIP) - iota((CHIP, 128), 0)).astype(F32)
    left64 = lane64 < CHIP
    lane32 = iota((32, 128), 1)
    q32 = lane32 % CHIP
    m32 = 2 * (q32 % 32) + q32 // 32
    spacing_y = (m32 - 2 * iota((32, 128), 0) - lane32 // CHIP).astype(F32)
    left32 = lane32 < CHIP
    decay = -1.0 / (2.0 * SIGMA * SIGMA)

    def prepare(i, carry):
        off_y = offs_s[0, i].astype(F32) * (1.0 / FIXED)
        off_x = offs_s[1, i].astype(F32) * (1.0 / FIXED)
        tops, bottoms = [], []
        for level in (-1.0, 0.0, 1.0):
            gap = spacing_x - (off_x + level)
            bell = jnp.exp(gap * gap * decay)
            tops.append(jnp.where(left64, bell, 0.0).astype(BF16))
            bottoms.append(jnp.where(left64, 0.0, bell).astype(BF16))
        wide = jnp.concatenate([jnp.concatenate(tops, axis=1), jnp.concatenate(bottoms, axis=1)], axis=0)
        own = held[0][lax.div(i, LINKS)]
        mbuf[i] = jnp.dot(own, wide, preferred_element_type=F32).astype(BF16)
        for e, level in enumerate((-1.0, 0.0, 1.0)):
            gap = spacing_y - (off_y + level)
            lhs[i, pl.ds(32 * e, 32), :] = jnp.exp(gap * gap * decay).astype(BF16)
        return carry

    def prepare_part(n):
        low = sum(PRE[:n])
        lax.fori_loop(low, low + PRE[n], prepare, 0)

    serve(0)
    prepare_part(0)
    for s in (1, 2, 3):
        for half in (0, 1):
            plus_arrived(s, half)
            if s < 3 or half == 0:
                plus_copy(s + 1, half).start()
            minus_arrived(s, half)
            if s < 3 or half == 1:
                minus_copy(s + 1, half).start()
        serve(2 * s - 1)
        serve(2 * s)
        prepare_part(s)
    for k in range(1, NZ):
        zsec_arrived(k)

    later = []
    for l in range(LINKS):
        dev = zsec[pl.ds(l, NZ, stride=8), :].astype(jnp.int32)
        pos = zsec[pl.ds(4 + l, NZ, stride=8), :].astype(jnp.int32)
        later.append((dev // ROW, (dev % ROW) * DATE_DEV + pos))
    down128 = iota((128, 128), 0)
    down8 = iota((8, 128), 0)
    for l in range(LINKS):
        for z in range(NZ):
            c = l * NZ + z
            hit = jnp.broadcast_to(later[l][1][z : z + 1, :], (128, 128)) == down128
            onehot[:, pl.ds(128 * c, 128)] = jnp.where(hit, 1.0, 0.0).astype(BF16)
            hit = jnp.broadcast_to(later[l][0][z : z + 1, :], (8, 128)) == down8
            member[pl.ds(8 * c, 8), :] = jnp.where(hit, 1.0, 0.0)

    plus_arrived(4, 0)
    minus_arrived(4, 1)
    serve(7)
    for t in range(NZ):
        for k in range(1, ROW):
            x_arrived(t, k, block_of(t))

    def score(i, carry):
        chip = recv[jnp.clip(req[8, i], 0, NZ * ROW * 2 - 1)].astype(F32)
        swapped = pltpu.roll(chip, CHIP, 1)
        blocks = jnp.concatenate(
            [
                jnp.where(left32, chip, 0.0).astype(BF16),
                jnp.where(left32, swapped, 0.0).astype(BF16),
                jnp.where(left32, 0.0, swapped).astype(BF16),
                jnp.where(left32, 0.0, chip).astype(BF16),
            ],
            axis=0,
        )
        lifted = jnp.dot(lhs[i], blocks, preferred_element_type=F32).astype(BF16).astype(F32)
        moved = mbuf[i].astype(F32)
        for ky in range(3):
            for kx in range(3):
                part = fold(lifted[32 * ky : 32 * ky + 32] * moved[:, 128 * kx : 128 * kx + 128])
                sums[pl.ds((3 * ky + kx) * PAIRS + i, 8, stride=ITEMS * PAIRS), :] = part
        sums[pl.ds(9 * PAIRS + i, 8, stride=ITEMS * PAIRS), :] = fold(chip * chip)
        sums[pl.ds(10 * PAIRS + i, 8, stride=ITEMS * PAIRS), :] = bnorm[pl.ds(8 * lax.div(i, LINKS), 8), :]
        return carry

    lax.fori_loop(0, PAIRS, score, 0)

    rows = []
    for item in range(ITEMS):
        part = sums[pl.ds(item * PAIRS, PAIRS), :]
        for s in range(1, 8):
            part = part + sums[pl.ds(s * ITEMS * PAIRS + item * PAIRS, PAIRS), :]
        rows.append(jnp.sum(part.T, axis=0, keepdims=True))
    size = CHIP / jnp.sqrt((rows[10] + EPS) * (rows[9] + EPS))
    scores = [rows[q] * size for q in range(9)]
    raised = [jnp.exp(ZSCALE * s) for s in scores]
    whole = raised[0]
    for q in range(1, 9):
        whole = whole + raised[q]
    weights = [r / whole for r in raised]
    offs = offs_v[...].astype(F32) * (1.0 / FIXED)
    move_y = offs[0:1] + ((weights[6] + weights[7] + weights[8]) - (weights[0] + weights[1] + weights[2]))
    move_x = offs[1:2] + ((weights[2] + weights[5] + weights[8]) - (weights[0] + weights[3] + weights[6]))
    blend = weights[0] * scores[0]
    for q in range(1, 9):
        blend = blend + weights[q] * scores[q]
    quality = 1.0 / (1.0 + jnp.exp(-ZSCALE * blend))
    measure_out[0] = move_y
    measure_out[1] = move_x
    measure_out[2] = quality

    up = jnp.where(r8 < 4, jnp.broadcast_to(move_y, (8, PAIRS)), jnp.broadcast_to(move_x, (8, PAIRS)))
    up = jnp.where(ours, up, 0.0)
    down = jnp.where(ours & (r8 < 4), jnp.broadcast_to(quality, (8, PAIRS)), 0.0)
    both = jnp.concatenate([up, down], axis=0)
    first = both.astype(BF16)
    rest = both - first.astype(F32)
    second = rest.astype(BF16)
    third = (rest - second.astype(F32)).astype(BF16)
    dealt = jnp.dot(jnp.concatenate([first, second, third], axis=0), deal, preferred_element_type=F32)
    mrow[pl.ds(0, 16), :] = dealt[0:16] + dealt[16:32] + dealt[32:48]

    def mrow_copy(k):
        return remote(mrow.at[pl.ds(0, 16)], mrow.at[pl.ds(16 * k, 16)], mrow_s.at[k], mrow_r.at[k], row_peer(k))

    for k in range(1, ROW):
        mrow_copy(k).start()
    for k in range(1, ROW):
        mrow_copy(k).wait_recv()
    total = mrow[pl.ds(0, 16), :]
    for k in range(1, ROW):
        total = total + mrow[pl.ds(16 * k, 16), :]
    mall[pl.ds(16 * mz, 16), :] = total

    def mall_copy(k):
        mine = mall.at[pl.ds(16 * mz, 16)]
        return remote(mine, mine, mall_s.at[k], mall_r.at[k], z_peer(k))

    def mall_arrived(k):
        theirs = mall.at[pl.ds(16 * lax.rem(mz - k + NZ, NZ), 16)]
        remote(theirs, theirs, mall_s.at[k], mall_r.at[k], z_peer(k)).wait_recv()

    for k in range(1, NZ):
        mall_copy(k).start()
    for k in range(1, NZ):
        mall_arrived(k)

    meas = [[mall[pl.ds(4 * a + l, NZ, stride=16), :] for l in range(LINKS)] for a in range(2)]
    qual = [mall[pl.ds(8 + l, NZ, stride=16), :] for l in range(LINKS)]
    field = None

    def halo_copy(n, side):
        return remote(
            fsend.at[pl.ds(16 * n, 16)],
            halo.at[pl.ds(16 * (2 * n + side), 16)],
            halo_s.at[n, side],
            halo_r.at[n, side],
            y_peer(1 if side == 0 else ny - 1),
        )

    for n, scale in enumerate(MUS):
        square = scale * scale
        numer = [None, None]
        denom = None
        for l in range(LINKS):
            if field is None:
                here = [0.0, 0.0]
                there = [0.0, 0.0]
            else:
                here = field
                there = []
                for a in range(2):
                    got = None
                    for z in range(NZ):
                        table = jnp.broadcast_to(field[a][z : z + 1, :], (NZ, 128))
                        found = jnp.take_along_axis(table, later[l][1], axis=1, mode="promise_in_bounds")
                        got = found if got is None else jnp.where(later[l][0] == z, found, got)
                    there.append(got)
            resid = [meas[a][l] - (there[a] - here[a]) for a in range(2)]
            gnc = qual[l] * square / (square + (resid[0] * resid[0] + resid[1] * resid[1]))
            values = [gnc * (here[a] + meas[a][l]) for a in range(2)] + [gnc]
            for a in range(2):
                back = gnc * (there[a] - meas[a][l])
                numer[a] = back if l == 0 else numer[a] + back
            denom = gnc if l == 0 else denom + gnc
            for z in range(NZ):
                c = l * NZ + z
                mask = member[pl.ds(8 * c, 8), :]
                tall = jnp.concatenate(
                    [jnp.broadcast_to(v[z : z + 1, :], (8, 128)) * mask for v in values], axis=0
                )
                high = tall.astype(BF16)
                low = (tall - high.astype(F32)).astype(BF16)
                spread[:, pl.ds(128 * c, 128)] = jnp.concatenate([high, low], axis=0)
        sent = lax.dot_general(
            spread[...], onehot[...], (((1,), (1,)), ((), ())), preferred_element_type=F32
        )
        sent = sent[0:24] + sent[24:48]
        numer = [numer[a] + sent[8 * a : 8 * a + 8] for a in range(2)]
        denom = denom + sent[16:24]
        if n > 0:
            for side in (0, 1):
                halo_copy(n - 1, side).wait_recv()
            base = 32 * (n - 1)
            below = [jnp.where(y > 0, halo[pl.ds(base + 8 * a, 8), :], 0.0) for a in range(2)]
            above = [jnp.where(y < ny - 1, halo[pl.ds(base + 16 + 8 * a, 8), :], 0.0) for a in range(2)]
            numer = [LAMBDA * (below[a] + above[a]) + numer[a] for a in range(2)]
        field = [numer[a] / (2.0 * LAMBDA + denom) for a in range(2)]
        if n < 2:
            for a in range(2):
                fsend[pl.ds(16 * n + 8 * a, 8), :] = field[a]
            for side in (0, 1):
                halo_copy(n, side).start()

    for a in range(2):
        mine = jnp.sum(jnp.where(down8 == mz, field[a], 0.0), axis=0, keepdims=True)
        turned = pltpu.roll(jnp.broadcast_to(mine, (8, 128)), lax.rem(128 - DATE_DEV * me, 128), 1)
        disp_out[a] = turned[0:1, :DATE_DEV]

    for k in range(1, ROW):
        row_copy(k).wait_send()
        mrow_copy(k).wait_send()
    for k in range(1, NZ):
        zsec_copy(k).wait_send()
        mall_copy(k).wait_send()
    for s in (1, 2, 3):
        for half in (0, 1):
            plus_copy(s, half).wait_send()
            minus_copy(s, half).wait_send()
    plus_copy(4, 0).wait_send()
    minus_copy(4, 1).wait_send()
    for t in range(NZ):
        for k in range(1, ROW):
            x_copy(t, k, block_of(t)).wait_send()
    for n in range(2):
        for side in (0, 1):
            halo_copy(n, side).wait_send()


def per_device(chips, pair_target, pair_slot, offset_fix):
    flat = chips.reshape(DATE_DEV, CHIP * CHIP)
    target = pair_target.reshape(1, PAIRS)
    slot = pair_slot.reshape(1, PAIRS)
    offs = jnp.transpose(offset_fix.reshape(PAIRS, 2), (1, 0))
    vmem = pl.BlockSpec(memory_space=pltpu.VMEM)
    smem = pl.BlockSpec(memory_space=pltpu.SMEM)
    dma = pltpu.SemaphoreType.DMA
    measure, disp = pl.pallas_call(
        kernel,
        out_shape=(
            jax.ShapeDtypeStruct((3, 1, PAIRS), F32),
            jax.ShapeDtypeStruct((2, 1, DATE_DEV), F32),
        ),
        in_specs=[vmem, vmem, vmem, smem, vmem],
        out_specs=(vmem, vmem),
        scratch_shapes=[
            pltpu.VMEM((DATE_DEV * 32 + 32, 128), F32),
            *[pltpu.VMEM((DATE_DEV, 32, 128), BF16)] * NZ,
            pltpu.VMEM((NZ * ROW * 2, 32, 128), BF16),
            pltpu.VMEM((NZ * ROW * 2, 32, 128), BF16),
            pltpu.VMEM((DATE_DEV * 8, 128), F32),
            pltpu.VMEM((ROW * 16 + 8, 128), F32),
            pltpu.VMEM((NZ * 8 + 8, 128), F32),
            pltpu.VMEM((16, 128), jnp.int32),
            pltpu.SMEM((16, 128), jnp.int32),
            pltpu.VMEM((PAIRS, 32, 384), BF16),
            pltpu.VMEM((PAIRS, 96, 128), BF16),
            pltpu.VMEM((128, LINKS * NZ * 128), BF16),
            pltpu.VMEM((LINKS * NZ * 8, 128), F32),
            pltpu.VMEM((9 * ITEMS * PAIRS, 128), F32),
            pltpu.VMEM((ROW * 16, 128), F32),
            pltpu.VMEM((NZ * 16 + 16, 128), F32),
            pltpu.VMEM((48, LINKS * NZ * 128), BF16),
            pltpu.VMEM((32, 128), F32),
            pltpu.VMEM((64, 128), F32),
            dma,
            dma((ROW,)),
            dma((ROW,)),
            dma((NZ,)),
            dma((NZ,)),
            dma((4, 2)),
            dma((4, 2)),
            dma((4, 2)),
            dma((4, 2)),
            dma((NZ, ROW)),
            dma((NZ, ROW)),
            dma((ROW,)),
            dma((ROW,)),
            dma((NZ,)),
            dma((NZ,)),
            dma((2, 2)),
            dma((2, 2)),
        ],
        compiler_params=pltpu.CompilerParams(
            collective_id=0, has_side_effects=True, vmem_limit_bytes=40 * 1024 * 1024
        ),
        name="offset_network",
    )(flat, target, slot, offs, offs)
    return (jnp.transpose(disp, (0, 2, 1)), jnp.transpose(measure, (0, 2, 1)))


def solution(mesh):
    in_specs = (P("date", "space", None), P("date", None), P("date"), P("date", "space", None))
    out_specs = (P(None, "date", "space"), P(None, "date", "space"))
    return jax.shard_map(
        per_device, mesh=mesh, in_specs=in_specs, out_specs=out_specs, check_vma=False
    )
```

time: 1000 us -> 74.8 us (0.07)
  blocking collectives: 833 us -> 0 us
  Pallas kernels: 0 us -> 70.6 us
  starting transfers between devices: 50.2 us -> 0 us
  local copies, waits for them, and re-layouts: 35.5 us -> 2.7 us
  waiting for transfers between devices: 30.7 us -> 0 us
  matrix products: 26.3 us -> 0 us
  other arithmetic: 15.4 us -> 0 us
    unnamed x3 -> x0, blocking collectives: 729 us -> none
    all_gather x2 -> x0, blocking collectives: 104 us -> none  [per_device(): everyone = lax.all_gather(field, 'date', axis=0, tiled=True)]
    pallas_call x0 -> x1, Pallas kernels: none -> 70.6 us  [per_device(): pl.pallas_call(kernel, out_shape=(jax.ShapeDtypeStruct((3, 1, PAIRS), F32...]
    all_to_all x4 -> x0, starting transfers between devices: 35.8 us -> none  [the longest x1 14.8 us: per_device(): lax.all_to_all(send_meta, 'date', split_axis=0, concat_axis=0, tiled=True)]
    all_to_all x4 -> x0, waiting for transfers between devices: 30.7 us -> none  [the longest x1 17.8 us: per_device(): lax.all_to_all(send_chips, 'date', split_axis=0, concat_axis=0, tiled=True)]
    dot_general x31 -> x0, matrix products: 26.3 us -> none  [the longest x8 14 us: correlate_rows(): jnp.einsum('qykn,qxkn->qyx', lifted, moved, preferred_element_type=jnp.fl...]
    ppermute x6 -> x0, starting transfers between devices: 14.4 us -> none  [the longest x3 10.4 us: padded_2(): lax.ppermute(tail, axis, [(i, (i + 1) % count) for i in range(ends)])]
  transfers between devices with their start and end apart: 10 -> 0, of which waited for: 3 -> 0; matrix products, arithmetic and copies ran while one was open for 7% -> 0% of each run, Pallas kernels for 0% -> 0%
where the time goes in v1:
time: 74.8 us; the launch traced here: 73.9 us
  Pallas kernels  70.6 us (94%)
  local copies, waits for them, and re-layouts  2.7 us (4%)
    pallas_call x1, Pallas kernels, per_device(): pl.pallas_call(kernel, out_shape=(jax.ShapeDtypeStruct((3, 1, PAIRS), F32...  70.6 us
    unnamed x10, local copies, waits for them, and re-layouts  2.7 us

profile of v1, /device:TPU:1, one launch (start us, length us, event | category | flops | bytes accessed | tf_op | source)
XLA Modules:
  0.0 73.9 jit_solution(17030004162010438478)
XLA Ops:
  0.6 0.0 copy-start.3
  0.6 0.0 copy-start.1
  0.7 0.0 copy-start.2
  0.7 0.6 copy-done.3
  1.3 0.0 copy-done.1
  1.3 0.0 copy-done.2
  1.3 0.0 copy-start
  1.3 0.9 %copy-done = bf16[16,1,4096]{2,0,1:T(8,128)(2,1)S(1)} copy-done((bf16[16,1,4096]{2,0,1:T(8,128)(2,1)S(1)}, bf16[16,1,4096]{2,0,1:T(8,128)(2,1)}, u32[]{:S(2)}) %copy-start) | copy-done | bytes 131096
  2.2 70.6 %offset_network.1 = (f32[3,1,64]{2,1,0:T(1,128)S(1)}, f32[2,1,16]{2,1,0:T(1,128)S(1)}) custom-call(bf16[16,4096]{1,0:T(8,128)(2,1)S(1)} %bitcast.10, s32[1,64]{1,0:T(1,128)S(1)} %bitcast.15, s32[1,64]{1,0:T(1,128)S(1)} %bitcast.16, s32[2,64]{1,0:T(2,128)S(1)} %bitcast.11, s32[2,64]{1,0:T(2,128)S(1)} %bitcast.12), custom_call_target="tpu_custom_call" | custom-call | tf_op jit(solution)/shard_map/offset_network/pallas_call | solution.py:500
  72.8 0.6 copy.9
  73.4 0.6 copy.10
Async XLA Ops:
  0.6 0.7 copy-start.3
  0.6 0.7 copy-start.1
  0.7 0.7 copy-start.2
  1.3 0.9 %copy-start = (bf16[16,1,4096]{2,0,1:T(8,128)(2,1)S(1)}, bf16[16,1,4096]{2,0,1:T(8,128)(2,1)}, u32[]{:S(2)}) copy-start(bf16[16,1,4096]{2,0,1:T(8,128)(2,1)} %param.4) | copy-start | bytes 393220

commit v2 on v1

--- a/solution.py
+++ b/solution.py
@@ -11,7 +11,8 @@
 NZ = 8
 DATE_DEV = 16
 PAIRS = 64
-HALF = 8
+CHUNKS = 4
+CHUNK = DATE_DEV // CHUNKS
 SIGMA = 0.6
 ZSCALE = 0.5
 EPS = 1e-06
@@ -21,7 +22,7 @@
 ITEMS = 11
 F32 = jnp.float32
 BF16 = jnp.bfloat16
-PRE = (16, 16, 16, 16)
+PRE = (6, 4, 3, 3)
 
 
 def iota(shape, dim):
@@ -38,13 +39,17 @@
 
 
 def kernel(
+    chips_in,
+    target_in,
+    slot_in,
+    offs_in,
+    measure_out,
+    disp_out,
     chips,
     target,
     slot,
     offs_s,
     offs_v,
-    measure_out,
-    disp_out,
     tmp,
     held0,
     held1,
@@ -71,6 +76,7 @@
     spread,
     fsend,
     halo,
+    sem_in,
     sem_req,
     row_s,
     row_r,
@@ -120,8 +126,19 @@
         pl.semaphore_signal(barrier, inc=1, device_id=row_peer(k), device_id_type=pl.DeviceIdType.MESH)
     for k in range(1, NZ):
         pl.semaphore_signal(barrier, inc=1, device_id=z_peer(k), device_id_type=pl.DeviceIdType.MESH)
-    for k in (1, ny - 1):
+    for k in (1, 2, ny - 2, ny - 1):
         pl.semaphore_signal(barrier, inc=1, device_id=y_peer(k), device_id_type=pl.DeviceIdType.MESH)
+
+    loads = [
+        pltpu.make_async_copy(src, dst, sem_in.at[n])
+        for n, (src, dst) in enumerate(
+            ((target_in, target), (slot_in, slot), (chips_in, chips), (offs_in, offs_s), (offs_in, offs_v))
+        )
+    ]
+    for load in loads:
+        load.start()
+    for load in loads:
+        load.wait()
 
     for j in range(32):
         tmp[pl.ds(j, DATE_DEV, stride=32), :] = chips[:, 128 * j : 128 * j + 128].astype(F32)
@@ -153,43 +170,78 @@
     rowx[pl.ds(0, 8), :] = jnp.dot(named, deal, preferred_element_type=F32)
     rowx[pl.ds(8, 8), :] = jnp.broadcast_to(wanted, (8, 128))
 
-    pl.semaphore_wait(barrier, ROW - 1 + NZ - 1 + 2)
+    pl.semaphore_wait(barrier, ROW - 1 + NZ - 1 + 4)
 
     def row_copy(k):
         return remote(rowx.at[pl.ds(0, 16)], rowx.at[pl.ds(16 * k, 16)], row_s.at[k], row_r.at[k], row_peer(k))
 
-    def ring_part(t, half):
-        return held[t].at[pl.ds(half * HALF, HALF)]
-
-    def plus_copy(s, half):
+    def ring_part(t, c):
+        return held[t].at[pl.ds(c * CHUNK, CHUNK)]
+
+    def plus_copy(s, c):
         return remote(
-            ring_part(max(2 * s - 3, 0), half),
-            ring_part(2 * s - 1, half),
-            plus_s.at[s - 1, half],
-            plus_r.at[s - 1, half],
+            ring_part(max(2 * s - 3, 0), c),
+            ring_part(2 * s - 1, c),
+            plus_s.at[s - 1, c],
+            plus_r.at[s - 1, c],
             z_peer(1),
         )
 
-    def minus_copy(s, half):
+    def minus_copy(s, c):
         return remote(
-            ring_part(2 * s - 2, half),
-            ring_part(min(2 * s, 7), half),
-            minus_s.at[s - 1, half],
-            minus_r.at[s - 1, half],
+            ring_part(2 * s - 2, c),
+            ring_part(min(2 * s, 7), c),
+            minus_s.at[s - 1, c],
+            minus_r.at[s - 1, c],
             z_peer(NZ - 1),
         )
 
-    def plus_arrived(s, half):
-        plus_copy(s, half).wait_recv()
-
-    def minus_arrived(s, half):
-        minus_copy(s, half).wait_recv()
+    def goes_plus(s, c):
+        return s < 4 or c < CHUNKS // 2
+
+    def goes_minus(s, c):
+        return s < 4 or c >= CHUNKS // 2
 
     for k in range(1, ROW):
         row_copy(k).start()
-    for half in (0, 1):
-        plus_copy(1, half).start()
-        minus_copy(1, half).start()
+    for c in range(CHUNKS):
+        plus_copy(1, c).start()
+        minus_copy(1, c).start()
+
+    lane64 = iota((CHIP, 128), 1)
+    spacing_x = ((lane64 % CHIP) - iota((CHIP, 128), 0)).astype(F32)
+    left64 = lane64 < CHIP
+    lane32 = iota((32, 128), 1)
+    q32 = lane32 % CHIP
+    m32 = 2 * (q32 % 32) + q32 // 32
+    spacing_y = (m32 - 2 * iota((32, 128), 0) - lane32 // CHIP).astype(F32)
+    left32 = lane32 < CHIP
+    decay = -1.0 / (2.0 * SIGMA * SIGMA)
+
+    def prepare(d, carry):
+        own = held[0][d]
+        for l in range(LINKS):
+            i = d * LINKS + l
+            off_y = offs_s[0, i].astype(F32) * (1.0 / FIXED)
+            off_x = offs_s[1, i].astype(F32) * (1.0 / FIXED)
+            tops, bottoms = [], []
+            for level in (-1.0, 0.0, 1.0):
+                gap = spacing_x - (off_x + level)
+                bell = jnp.exp(gap * gap * decay)
+                tops.append(jnp.where(left64, bell, 0.0).astype(BF16))
+                bottoms.append(jnp.where(left64, 0.0, bell).astype(BF16))
+            wide = jnp.concatenate([jnp.concatenate(tops, axis=1), jnp.concatenate(bottoms, axis=1)], axis=0)
+            mbuf[i] = jnp.dot(own, wide, preferred_element_type=F32).astype(BF16)
+            for e, level in enumerate((-1.0, 0.0, 1.0)):
+                gap = spacing_y - (off_y + level)
+                lhs[i, pl.ds(32 * e, 32), :] = jnp.exp(gap * gap * decay).astype(BF16)
+        return carry
+
+    def prepare_part(n):
+        low = sum(PRE[:n])
+        lax.fori_loop(low, low + PRE[n], prepare, 0)
+
+    prepare_part(0)
     for k in range(1, ROW):
         row_copy(k).wait_recv()
 
@@ -210,8 +262,6 @@
         theirs = zsec.at[pl.ds(8 * lax.rem(mz - k + NZ, NZ), 8)]
         remote(theirs, theirs, zsec_s.at[k], zsec_r.at[k], z_peer(k)).wait_recv()
 
-    for k in range(1, NZ):
-        zsec_copy(k).start()
     fetch.wait()
 
     def x_copy(t, k, block):
@@ -244,47 +294,17 @@
             if k:
                 x_copy(t, k, block).start()
 
-    lane64 = iota((CHIP, 128), 1)
-    spacing_x = ((lane64 % CHIP) - iota((CHIP, 128), 0)).astype(F32)
-    left64 = lane64 < CHIP
-    lane32 = iota((32, 128), 1)
-    q32 = lane32 % CHIP
-    m32 = 2 * (q32 % 32) + q32 // 32
-    spacing_y = (m32 - 2 * iota((32, 128), 0) - lane32 // CHIP).astype(F32)
-    left32 = lane32 < CHIP
-    decay = -1.0 / (2.0 * SIGMA * SIGMA)
-
-    def prepare(i, carry):
-        off_y = offs_s[0, i].astype(F32) * (1.0 / FIXED)
-        off_x = offs_s[1, i].astype(F32) * (1.0 / FIXED)
-        tops, bottoms = [], []
-        for level in (-1.0, 0.0, 1.0):
-            gap = spacing_x - (off_x + level)
-            bell = jnp.exp(gap * gap * decay)
-            tops.append(jnp.where(left64, bell, 0.0).astype(BF16))
-            bottoms.append(jnp.where(left64, 0.0, bell).astype(BF16))
-        wide = jnp.concatenate([jnp.concatenate(tops, axis=1), jnp.concatenate(bottoms, axis=1)], axis=0)
-        own = held[0][lax.div(i, LINKS)]
-        mbuf[i] = jnp.dot(own, wide, preferred_element_type=F32).astype(BF16)
-        for e, level in enumerate((-1.0, 0.0, 1.0)):
-            gap = spacing_y - (off_y + level)
-            lhs[i, pl.ds(32 * e, 32), :] = jnp.exp(gap * gap * decay).astype(BF16)
-        return carry
-
-    def prepare_part(n):
-        low = sum(PRE[:n])
-        lax.fori_loop(low, low + PRE[n], prepare, 0)
-
     serve(0)
-    prepare_part(0)
+    for k in range(1, NZ):
+        zsec_copy(k).start()
     for s in (1, 2, 3):
-        for half in (0, 1):
-            plus_arrived(s, half)
-            if s < 3 or half == 0:
-                plus_copy(s + 1, half).start()
-            minus_arrived(s, half)
-            if s < 3 or half == 1:
-                minus_copy(s + 1, half).start()
+        for c in range(CHUNKS):
+            plus_copy(s, c).wait_recv()
+            if goes_plus(s + 1, c):
+                plus_copy(s + 1, c).start()
+            minus_copy(s, c).wait_recv()
+            if goes_minus(s + 1, c):
+                minus_copy(s + 1, c).start()
         serve(2 * s - 1)
         serve(2 * s)
         prepare_part(s)
@@ -306,36 +326,41 @@
             hit = jnp.broadcast_to(later[l][0][z : z + 1, :], (8, 128)) == down8
             member[pl.ds(8 * c, 8), :] = jnp.where(hit, 1.0, 0.0)
 
-    plus_arrived(4, 0)
-    minus_arrived(4, 1)
+    for c in range(CHUNKS):
+        (plus_copy if goes_plus(4, c) else minus_copy)(4, c).wait_recv()
     serve(7)
     for t in range(NZ):
         for k in range(1, ROW):
             x_arrived(t, k, block_of(t))
 
-    def score(i, carry):
-        chip = recv[jnp.clip(req[8, i], 0, NZ * ROW * 2 - 1)].astype(F32)
-        swapped = pltpu.roll(chip, CHIP, 1)
-        blocks = jnp.concatenate(
-            [
-                jnp.where(left32, chip, 0.0).astype(BF16),
-                jnp.where(left32, swapped, 0.0).astype(BF16),
-                jnp.where(left32, 0.0, swapped).astype(BF16),
-                jnp.where(left32, 0.0, chip).astype(BF16),
-            ],
-            axis=0,
-        )
-        lifted = jnp.dot(lhs[i], blocks, preferred_element_type=F32).astype(BF16).astype(F32)
-        moved = mbuf[i].astype(F32)
-        for ky in range(3):
-            for kx in range(3):
-                part = fold(lifted[32 * ky : 32 * ky + 32] * moved[:, 128 * kx : 128 * kx + 128])
-                sums[pl.ds((3 * ky + kx) * PAIRS + i, 8, stride=ITEMS * PAIRS), :] = part
-        sums[pl.ds(9 * PAIRS + i, 8, stride=ITEMS * PAIRS), :] = fold(chip * chip)
-        sums[pl.ds(10 * PAIRS + i, 8, stride=ITEMS * PAIRS), :] = bnorm[pl.ds(8 * lax.div(i, LINKS), 8), :]
+    def score(d, carry):
+        pairs = [d * LINKS + l for l in range(LINKS)]
+        chip = [recv[jnp.clip(req[8, i], 0, NZ * ROW * 2 - 1)].astype(F32) for i in pairs]
+        lifted = []
+        for l, i in enumerate(pairs):
+            swapped = pltpu.roll(chip[l], CHIP, 1)
+            blocks = jnp.concatenate(
+                [
+                    jnp.where(left32, chip[l], 0.0).astype(BF16),
+                    jnp.where(left32, swapped, 0.0).astype(BF16),
+                    jnp.where(left32, 0.0, swapped).astype(BF16),
+                    jnp.where(left32, 0.0, chip[l]).astype(BF16),
+                ],
+                axis=0,
+            )
+            lifted.append(jnp.dot(lhs[i], blocks, preferred_element_type=F32).astype(BF16))
+        for l, i in enumerate(pairs):
+            up = lifted[l].astype(F32)
+            moved = mbuf[i].astype(F32)
+            for ky in range(3):
+                for kx in range(3):
+                    part = fold(up[32 * ky : 32 * ky + 32] * moved[:, 128 * kx : 128 * kx + 128])
+                    sums[pl.ds((3 * ky + kx) * PAIRS + i, 8, stride=ITEMS * PAIRS), :] = part
+            sums[pl.ds(9 * PAIRS + i, 8, stride=ITEMS * PAIRS), :] = fold(chip[l] * chip[l])
+            sums[pl.ds(10 * PAIRS + i, 8, stride=ITEMS * PAIRS), :] = bnorm[pl.ds(8 * d, 8), :]
         return carry
 
-    lax.fori_loop(0, PAIRS, score, 0)
+    lax.fori_loop(0, DATE_DEV, score, 0)
 
     rows = []
     for item in range(ITEMS):
@@ -402,13 +427,16 @@
     field = None
 
     def halo_copy(n, side):
-        return remote(
-            fsend.at[pl.ds(16 * n, 16)],
-            halo.at[pl.ds(16 * (2 * n + side), 16)],
-            halo_s.at[n, side],
-            halo_r.at[n, side],
-            y_peer(1 if side == 0 else ny - 1),
-        )
+        peer = y_peer((1, ny - 1, 2, ny - 2)[side])
+        if n == 0:
+            return remote(fsend.at[pl.ds(0, 16)], halo.at[side, pl.ds(0, 16)], halo_s.at[0, side], halo_r.at[0, side], peer)
+        return remote(fsend.at[pl.ds(16, 24)], halo.at[side, pl.ds(16, 24)], halo_s.at[1, side], halo_r.at[1, side], peer)
+
+    def inside(steps, value):
+        return jnp.where((y + steps >= 0) & (y + steps < ny), value, 0.0)
+
+    def settle(beside, numer, denom):
+        return [(LAMBDA * beside[a] + numer[a]) / (2.0 * LAMBDA + denom) for a in range(2)]
 
     for n, scale in enumerate(MUS):
         square = scale * scale
@@ -450,19 +478,33 @@
         sent = sent[0:24] + sent[24:48]
         numer = [numer[a] + sent[8 * a : 8 * a + 8] for a in range(2)]
         denom = denom + sent[16:24]
-        if n > 0:
+        if n == 0:
+            field = [numer[a] / (2.0 * LAMBDA + denom) for a in range(2)]
+            for a in range(2):
+                fsend[pl.ds(8 * a, 8), :] = field[a]
+            for side in range(4):
+                halo_copy(0, side).start()
+        elif n == 1:
+            for a in range(2):
+                fsend[pl.ds(16 + 8 * a, 8), :] = numer[a]
+            fsend[pl.ds(32, 8), :] = denom
             for side in (0, 1):
-                halo_copy(n - 1, side).wait_recv()
-            base = 32 * (n - 1)
-            below = [jnp.where(y > 0, halo[pl.ds(base + 8 * a, 8), :], 0.0) for a in range(2)]
-            above = [jnp.where(y < ny - 1, halo[pl.ds(base + 16 + 8 * a, 8), :], 0.0) for a in range(2)]
-            numer = [LAMBDA * (below[a] + above[a]) + numer[a] for a in range(2)]
-        field = [numer[a] / (2.0 * LAMBDA + denom) for a in range(2)]
-        if n < 2:
-            for a in range(2):
-                fsend[pl.ds(16 * n + 8 * a, 8), :] = field[a]
+                halo_copy(1, side).start()
+            for side in range(4):
+                halo_copy(0, side).wait_recv()
+            near = [inside(-1, halo[0, pl.ds(8 * a, 8), :]) + inside(1, halo[1, pl.ds(8 * a, 8), :]) for a in range(2)]
+            start = field
+            field = settle(near, numer, denom)
+        else:
             for side in (0, 1):
-                halo_copy(n, side).start()
+                halo_copy(1, side).wait_recv()
+            beside = [0.0, 0.0]
+            for side, way in ((0, -1), (1, 1)):
+                reach = [start[a] + inside(2 * way, halo[2 + side, pl.ds(8 * a, 8), :]) for a in range(2)]
+                theirs = [halo[side, pl.ds(16 + 8 * a, 8), :] for a in range(2)]
+                there = settle(reach, theirs, halo[side, pl.ds(32, 8), :])
+                beside = [beside[a] + inside(way, there[a]) for a in range(2)]
+            field = settle(beside, numer, denom)
 
     for a in range(2):
         mine = jnp.sum(jnp.where(down8 == mz, field[a], 0.0), axis=0, keepdims=True)
@@ -475,18 +517,17 @@
     for k in range(1, NZ):
         zsec_copy(k).wait_send()
         mall_copy(k).wait_send()
-    for s in (1, 2, 3):
-        for half in (0, 1):
-            plus_copy(s, half).wait_send()
-            minus_copy(s, half).wait_send()
-    plus_copy(4, 0).wait_send()
-    minus_copy(4, 1).wait_send()
+    for s in (1, 2, 3, 4):
+        for c in range(CHUNKS):
+            if goes_plus(s, c):
+                plus_copy(s, c).wait_send()
+            if goes_minus(s, c):
+                minus_copy(s, c).wait_send()
     for t in range(NZ):
         for k in range(1, ROW):
             x_copy(t, k, block_of(t)).wait_send()
-    for n in range(2):
-        for side in (0, 1):
-            halo_copy(n, side).wait_send()
+    for n, side in ((0, 0), (0, 1), (0, 2), (0, 3), (1, 0), (1, 1)):
+        halo_copy(n, side).wait_send()
 
 
 def per_device(chips, pair_target, pair_slot, offset_fix):
@@ -495,7 +536,7 @@
     slot = pair_slot.reshape(1, PAIRS)
     offs = jnp.transpose(offset_fix.reshape(PAIRS, 2), (1, 0))
     vmem = pl.BlockSpec(memory_space=pltpu.VMEM)
-    smem = pl.BlockSpec(memory_space=pltpu.SMEM)
+    anywhere = pl.BlockSpec(memory_space=pl.ANY)
     dma = pltpu.SemaphoreType.DMA
     measure, disp = pl.pallas_call(
         kernel,
@@ -503,9 +544,14 @@
             jax.ShapeDtypeStruct((3, 1, PAIRS), F32),
             jax.ShapeDtypeStruct((2, 1, DATE_DEV), F32),
         ),
-        in_specs=[vmem, vmem, vmem, smem, vmem],
+        in_specs=[anywhere] * 4,
         out_specs=(vmem, vmem),
         scratch_shapes=[
+            pltpu.VMEM((DATE_DEV, CHIP * CHIP), BF16),
+            pltpu.VMEM((1, PAIRS), jnp.int32),
+            pltpu.VMEM((1, PAIRS), jnp.int32),
+            pltpu.SMEM((2, PAIRS), jnp.int32),
+            pltpu.VMEM((2, PAIRS), jnp.int32),
             pltpu.VMEM((DATE_DEV * 32 + 32, 128), F32),
             *[pltpu.VMEM((DATE_DEV, 32, 128), BF16)] * NZ,
             pltpu.VMEM((NZ * ROW * 2, 32, 128), BF16),
@@ -523,31 +569,32 @@
             pltpu.VMEM((ROW * 16, 128), F32),
             pltpu.VMEM((NZ * 16 + 16, 128), F32),
             pltpu.VMEM((48, LINKS * NZ * 128), BF16),
-            pltpu.VMEM((32, 128), F32),
-            pltpu.VMEM((64, 128), F32),
+            pltpu.VMEM((40, 128), F32),
+            pltpu.VMEM((4, 40, 128), F32),
+            dma((5,)),
             dma,
             dma((ROW,)),
             dma((ROW,)),
             dma((NZ,)),
             dma((NZ,)),
-            dma((4, 2)),
-            dma((4, 2)),
-            dma((4, 2)),
-            dma((4, 2)),
+            dma((4, CHUNKS)),
+            dma((4, CHUNKS)),
+            dma((4, CHUNKS)),
+            dma((4, CHUNKS)),
             dma((NZ, ROW)),
             dma((NZ, ROW)),
             dma((ROW,)),
             dma((ROW,)),
             dma((NZ,)),
             dma((NZ,)),
-            dma((2, 2)),
-            dma((2, 2)),
+            dma((2, 4)),
+            dma((2, 4)),
         ],
         compiler_params=pltpu.CompilerParams(
             collective_id=0, has_side_effects=True, vmem_limit_bytes=40 * 1024 * 1024
         ),
         name="offset_network",
-    )(flat, target, slot, offs, offs)
+    )(flat, target, slot, offs)
     return (jnp.transpose(disp, (0, 2, 1)), jnp.transpose(measure, (0, 2, 1)))
 
 

time: 74.8 us -> 60.9 us (0.81)
  Pallas kernels: 70.6 us -> 57.2 us
    pallas_call x1, Pallas kernels: 70.6 us -> 57.2 us  [per_device(): pl.pallas_call(kernel, out_shape=(jax.ShapeDtypeStruct((3, 1, PAIRS), F32...]
where the time goes in v2:
time: 60.9 us; the launch traced here: 60.6 us
  Pallas kernels  57.2 us (94%)
  local copies, waits for them, and re-layouts  2.7 us (4%)
  between operations  0.67 us (1%)
    pallas_call x1, Pallas kernels, per_device(): pl.pallas_call(kernel, out_shape=(jax.ShapeDtypeStruct((3, 1, PAIRS), F32...  57.2 us
    unnamed x10, local copies, waits for them, and re-layouts  2.7 us

profile of v2, /device:TPU:1, one launch (start us, length us, event | category | flops | bytes accessed | tf_op | source)
XLA Modules:
  0.0 60.6 jit_solution(12819732197527857199)
XLA Ops:
  0.6 0.0 copy-start.3
  0.6 0.0 copy-start.1
  0.7 0.0 copy-start.2
  0.7 0.6 %copy-done.3 = s32[64]{0:T(128)S(1)} copy-done((s32[64]{0:T(128)S(1)}, s32[64]{0:T(128)}, u32[]{:S(2)}) %copy-start.3) | copy-done | bytes 280
  1.3 0.0 copy-done.1
  1.3 0.0 copy-done.2
  1.3 0.0 copy-start
  1.3 0.9 %copy-done = bf16[16,1,4096]{2,0,1:T(8,128)(2,1)S(1)} copy-done((bf16[16,1,4096]{2,0,1:T(8,128)(2,1)S(1)}, bf16[16,1,4096]{2,0,1:T(8,128)(2,1)}, u32[]{:S(2)}) %copy-start) | copy-done | bytes 131096
  2.2 57.2 %offset_network.1 = (f32[3,1,64]{2,1,0:T(1,128)S(1)}, f32[2,1,16]{2,1,0:T(1,128)S(1)}) custom-call(bf16[16,4096]{1,0:T(8,128)(2,1)S(1)} %bitcast.10, s32[1,64]{1,0:T(1,128)S(1)} %bitcast.14, s32[1,64]{1,0:T(1,128)S(1)} %bitcast.15, s32[2,64]{1,0:T(2,128)S(1)} %bitcast.12), custom_call_target="tpu_custom_call" | custom-call | tf_op jit(solution)/shard_map/offset_network/pallas_call | solution.py:541
  59.5 0.6 copy.9
  60.0 0.6 copy.10
Async XLA Ops:
  0.6 0.7 %copy-start.3 = (s32[64]{0:T(128)S(1)}, s32[64]{0:T(128)}, u32[]{:S(2)}) copy-start(s32[64]{0:T(128)} %param.6) | copy-start | bytes 772
  0.6 0.7 %copy-start.1 = (s32[64,1,2]{0,2,1:T(2,128)S(1)}, s32[64,1,2]{0,2,1:T(2,128)}, u32[]{:S(2)}) copy-start(s32[64,1,2]{0,2,1:T(2,128)} %param.7) | copy-start | bytes 1540
  0.7 0.7 %copy-start.2 = (s32[64,1]{0,1:T(1,128)S(1)}, s32[64,1]{0,1:T(1,128)}, u32[]{:S(2)}) copy-start(s32[64,1]{0,1:T(1,128)} %param.5) | copy-start | bytes 772
  1.3 0.9 %copy-start = (bf16[16,1,4096]{2,0,1:T(8,128)(2,1)S(1)}, bf16[16,1,4096]{2,0,1:T(8,128)(2,1)}, u32[]{:S(2)}) copy-start(bf16[16,1,4096]{2,0,1:T(8,128)(2,1)} %param.4) | copy-start | bytes 393220

commit v3 on v2

--- a/solution.py
+++ b/solution.py
@@ -22,7 +22,9 @@
 ITEMS = 11
 F32 = jnp.float32
 BF16 = jnp.bfloat16
-PRE = (6, 4, 3, 3)
+PRE = (7, 1, 2, 2, 4)
+SLOTS = 128
+GROUPS = ((0,), (1, 2), (3, 4), (5, 6), (7,))
 
 
 def iota(shape, dim):
@@ -33,9 +35,14 @@
     return jnp.sum(rows.reshape(rows.shape[0] // 8, 8, 128), axis=0)
 
 
-def split_bf16(value):
-    high = value.astype(BF16)
-    return high, (value - high.astype(F32)).astype(BF16)
+def thirds_dot(value, chosen):
+    first = value.astype(BF16)
+    rest = value - first.astype(F32)
+    second = rest.astype(BF16)
+    third = (rest - second.astype(F32)).astype(BF16)
+    out = jnp.dot(jnp.concatenate([first, second, third], axis=0), chosen, preferred_element_type=F32)
+    n = value.shape[0]
+    return out[:n] + out[n : 2 * n] + out[2 * n :]
 
 
 def kernel(
@@ -132,20 +139,13 @@
     loads = [
         pltpu.make_async_copy(src, dst, sem_in.at[n])
         for n, (src, dst) in enumerate(
-            ((target_in, target), (slot_in, slot), (chips_in, chips), (offs_in, offs_s), (offs_in, offs_v))
+            ((chips_in, chips), (target_in, target), (slot_in, slot), (offs_in, offs_s), (offs_in, offs_v))
         )
     ]
     for load in loads:
         load.start()
-    for load in loads:
+    for load in loads[1:]:
         load.wait()
-
-    for j in range(32):
-        tmp[pl.ds(j, DATE_DEV, stride=32), :] = chips[:, 128 * j : 128 * j + 128].astype(F32)
-    for d in range(DATE_DEV):
-        own = tmp[pl.ds(32 * d, 32), :]
-        held[0][d] = own.astype(BF16)
-        bnorm[pl.ds(8 * d, 8), :] = fold(own * own)
 
     sub = iota((PAIRS, 128), 0)
     lane = iota((PAIRS, 128), 1)
@@ -158,9 +158,14 @@
     tcol = jnp.sum(jnp.where(eye, tb, 0.0), axis=1, keepdims=True)
     scol = jnp.sum(jnp.where(eye, sb, 0.0), axis=1, keepdims=True)
     twin = jnp.where((tcol == tb) & (lane < sub), 1.0, 0.0)
-    place = 2.0 * tcol + jnp.sum(twin, axis=1, keepdims=True)
-    wanted = jnp.sum(jnp.where(lane.astype(F32) == place, scol, 0.0), axis=0, keepdims=True)
-    place_row = jnp.sum(jnp.where(eye, place, 0.0), axis=0, keepdims=True)
+    rank = jnp.sum(twin, axis=1, keepdims=True).astype(jnp.int32)
+    holder = tcol.astype(jnp.int32)
+    away = (holder // ROW - mz + NZ) % NZ
+    turn = jnp.where(away < NZ // 2, 2 * away, 2 * NZ - 1 - 2 * away)
+    place = turn * (2 * ROW) + (holder % ROW) * 2 + rank
+    wanted = jnp.sum(jnp.where(lane == place, scol, 0.0), axis=0, keepdims=True)
+    pair_of = jnp.sum(jnp.where(lane == place, sub.astype(F32), 0.0), axis=0, keepdims=True)
+    place_row = jnp.sum(jnp.where(eye, place.astype(F32), 0.0), axis=0, keepdims=True)
     deal = jnp.where(lane == me * DATE_DEV + sub // LINKS, 1.0, 0.0).astype(BF16)
     r8 = iota((8, PAIRS), 0)
     l8 = iota((8, PAIRS), 1)
@@ -170,6 +175,14 @@
     rowx[pl.ds(0, 8), :] = jnp.dot(named, deal, preferred_element_type=F32)
     rowx[pl.ds(8, 8), :] = jnp.broadcast_to(wanted, (8, 128))
 
+    loads[0].wait()
+    for j in range(32):
+        tmp[pl.ds(j, DATE_DEV, stride=32), :] = chips[:, 128 * j : 128 * j + 128].astype(F32)
+    for d in range(DATE_DEV):
+        own = tmp[pl.ds(32 * d, 32), :]
+        held[0][d] = own.astype(BF16)
+        bnorm[d] = fold(own * own)
+
     pl.semaphore_wait(barrier, ROW - 1 + NZ - 1 + 4)
 
     def row_copy(k):
@@ -202,11 +215,12 @@
     def goes_minus(s, c):
         return s < 4 or c >= CHUNKS // 2
 
-    for k in range(1, ROW):
-        row_copy(k).start()
     for c in range(CHUNKS):
         plus_copy(1, c).start()
         minus_copy(1, c).start()
+        if c == 0:
+            for k in range(1, ROW):
+                row_copy(k).start()
 
     lane64 = iota((CHIP, 128), 1)
     spacing_x = ((lane64 % CHIP) - iota((CHIP, 128), 0)).astype(F32)
@@ -241,73 +255,174 @@
         low = sum(PRE[:n])
         lax.fori_loop(low, low + PRE[n], prepare, 0)
 
-    prepare_part(0)
-    for k in range(1, ROW):
-        row_copy(k).wait_recv()
-
-    reqv[pl.ds(0, 8), :] = rowx[pl.ds(8, 8, stride=16), :].astype(jnp.int32)
-    reqv[pl.ds(8, 8), :] = jnp.broadcast_to(place_row, (8, 128)).astype(jnp.int32)
-    fetch = pltpu.make_async_copy(reqv, req, sem_req)
-    fetch.start()
-    total = rowx[pl.ds(0, 8), :]
-    for k in range(1, ROW):
-        total = total + rowx[pl.ds(16 * k, 8), :]
-    zsec[pl.ds(8 * mz, 8), :] = total
-
-    def zsec_copy(k):
-        mine = zsec.at[pl.ds(8 * mz, 8)]
-        return remote(mine, mine, zsec_s.at[k], zsec_r.at[k], z_peer(k))
-
-    def zsec_arrived(k):
-        theirs = zsec.at[pl.ds(8 * lax.rem(mz - k + NZ, NZ), 8)]
-        remote(theirs, theirs, zsec_s.at[k], zsec_r.at[k], z_peer(k)).wait_recv()
-
-    fetch.wait()
-
-    def x_copy(t, k, block):
-        return remote(
-            xsend.at[pl.ds((t * ROW + k) * 2, 2)],
-            recv.at[pl.ds(block * 16 + me * 2, 2)],
-            x_s.at[t, k],
-            x_r.at[t, k],
-            row_peer(k),
-        )
-
-    def x_arrived(t, k, block):
-        theirs = recv.at[pl.ds(block * 16 + lax.rem(me - k + ROW, ROW) * 2, 2)]
-        remote(xsend.at[pl.ds((t * ROW + k) * 2, 2)], theirs, x_s.at[t, k], x_r.at[t, k], row_peer(k)).wait_recv()
-
-    def block_of(t):
-        step = (t + 1) // 2
-        return lax.rem(mz - step + NZ, NZ) if t % 2 else lax.rem(mz + step, NZ)
-
-    def serve(t):
-        block = block_of(t)
-        for k in (1, 7, 2, 6, 3, 5, 4, 0):
-            asker = (ROW - k) % ROW
-            for r in (0, 1):
-                chip = held[t][jnp.clip(req[asker, block * 16 + me * 2 + r], 0, DATE_DEV - 1)]
-                if k:
-                    xsend[(t * ROW + k) * 2 + r] = chip
-                else:
-                    recv[block * 16 + me * 2 + r] = chip
-            if k:
-                x_copy(t, k, block).start()
-
-    serve(0)
-    for k in range(1, NZ):
-        zsec_copy(k).start()
-    for s in (1, 2, 3):
-        for c in range(CHUNKS):
+    def forward(s, chunks):
+        for c in chunks:
             plus_copy(s, c).wait_recv()
             if goes_plus(s + 1, c):
                 plus_copy(s + 1, c).start()
             minus_copy(s, c).wait_recv()
             if goes_minus(s + 1, c):
                 minus_copy(s + 1, c).start()
-        serve(2 * s - 1)
-        serve(2 * s)
+
+    prepare_part(0)
+    forward(1, range(2))
+    for k in range(1, ROW):
+        row_copy(k).wait_recv()
+    reqv[pl.ds(0, 8), :] = rowx[pl.ds(8, 8, stride=16), :].astype(jnp.int32)
+    reqv[pl.ds(8, 8), :] = jnp.broadcast_to(pair_of, (8, 128)).astype(jnp.int32)
+    fetch = pltpu.make_async_copy(reqv, req, sem_req)
+    fetch.start()
+    forward(1, range(2, CHUNKS))
+    fetch.wait()
+    total = rowx[pl.ds(0, 8), :]
+    for k in range(1, ROW):
+        total = total + rowx[pl.ds(16 * k, 8), :]
+    zsec[pl.ds(8 * mz, 8), :] = total
+
+    def zsec_copy(k):
+        mine = zsec.at[pl.ds(8 * mz, 8)]
+        return remote(mine, mine, zsec_s.at[k], zsec_r.at[k], z_peer(k))
+
+    def zsec_arrived(k):
+        theirs = zsec.at[pl.ds(8 * lax.rem(mz - k + NZ, NZ), 8)]
+        remote(theirs, theirs, zsec_s.at[k], zsec_r.at[k], z_peer(k)).wait_recv()
+
+    def x_copy(g, k):
+        first, count = GROUPS[g][0], len(GROUPS[g])
+        return remote(
+            xsend.at[k, pl.ds(first, count)],
+            recv.at[pl.ds(first, count), me],
+            x_s.at[g, k],
+            x_r.at[g, k],
+            row_peer(k),
+        )
+
+    def x_arrived(g, k):
+        first, count = GROUPS[g][0], len(GROUPS[g])
+        theirs = recv.at[pl.ds(first, count), lax.rem(me - k + ROW, ROW)]
+        remote(xsend.at[k, pl.ds(first, count)], theirs, x_s.at[g, k], x_r.at[g, k], row_peer(k)).wait_recv()
+
+    def serve(g):
+        for k in (4, 3, 5, 2, 6, 1, 7, 0):
+            asker = (ROW - k) % ROW
+            for t in GROUPS[g]:
+                for r in (0, 1):
+                    chip = held[t][jnp.clip(req[asker, t * 2 * ROW + me * 2 + r], 0, DATE_DEV - 1)]
+                    if k:
+                        xsend[k, t, r] = chip
+                    else:
+                        recv[t, me, r] = chip
+            if k:
+                x_copy(g, k).start()
+
+    serve(0)
+    serve(1)
+    for k in range(1, NZ):
+        zsec_copy(k).start()
+    prepare_part(1)
+    for s in (2, 3):
+        forward(s, range(CHUNKS))
+        serve(s)
         prepare_part(s)
+    for c in range(CHUNKS):
+        (plus_copy if goes_plus(4, c) else minus_copy)(4, c).wait_recv()
+    serve(4)
+    prepare_part(4)
+
+    sub8 = iota((8, 128), 0)
+    lane8 = iota((8, 128), 1)
+
+    def fold8(parts):
+        once = [
+            jnp.where(sub8 < 4, parts[j], parts[j + 4])
+            + pltpu.roll(jnp.where(sub8 < 4, parts[j + 4], parts[j]), 4, 0)
+            for j in range(4)
+        ]
+
+        def pair(a, b, n):
+            return jnp.where(sub8 % (2 * n) < n, a + pltpu.roll(a, 8 - n, 0), b + pltpu.roll(b, n, 0))
+
+        return pair(pair(once[0], once[2], 2), pair(once[1], once[3], 2), 1)
+
+    def score(t, part):
+        slots = [t * 2 * ROW + part * 8 + j for j in range(8)]
+        pairs = [jnp.clip(req[8, slot], 0, PAIRS - 1) for slot in slots]
+        chip = [recv[t, part * 4 + j // 2, j % 2].astype(F32) for j in range(8)]
+        lifted = []
+        for j in range(8):
+            swapped = pltpu.roll(chip[j], CHIP, 1)
+            blocks = jnp.concatenate(
+                [
+                    jnp.where(left32, chip[j], 0.0).astype(BF16),
+                    jnp.where(left32, swapped, 0.0).astype(BF16),
+                    jnp.where(left32, 0.0, swapped).astype(BF16),
+                    jnp.where(left32, 0.0, chip[j]).astype(BF16),
+                ],
+                axis=0,
+            )
+            lifted.append(jnp.dot(lhs[pairs[j]], blocks, preferred_element_type=F32).astype(BF16))
+        items = [[] for _ in range(ITEMS)]
+        for j in range(8):
+            up = lifted[j].astype(F32)
+            moved = mbuf[pairs[j]].astype(F32)
+            for ky in range(3):
+                for kx in range(3):
+                    items[3 * ky + kx].append(fold(up[32 * ky : 32 * ky + 32] * moved[:, 128 * kx : 128 * kx + 128]))
+            items[9].append(fold(chip[j] * chip[j]))
+            items[10].append(bnorm[lax.div(pairs[j], LINKS)])
+        table = jnp.zeros((8, 128), F32)
+        for item in range(ITEMS):
+            table = jnp.where(lane8 == item, jnp.sum(fold8(items[item]), axis=1, keepdims=True), table)
+        sums[pl.ds(pl.multiple_of(t * 2 * ROW + part * 8, 8), 8), :] = table
+
+    for g in range(len(GROUPS)):
+        for k in range(1, ROW):
+            x_arrived(g, k)
+        first, count = GROUPS[g][0], len(GROUPS[g])
+
+        def score_step(n, carry, first=first):
+            score(first + lax.div(n, 2), lax.rem(n, 2))
+            return carry
+
+        lax.fori_loop(0, 2 * count, score_step, 0)
+
+    turned = sums[...].T
+    rows = [turned[item : item + 1, :] for item in range(ITEMS)]
+    size = CHIP / jnp.sqrt((rows[10] + EPS) * (rows[9] + EPS))
+    scores = [rows[q] * size for q in range(9)]
+    raised = [jnp.exp(ZSCALE * s) for s in scores]
+    whole = raised[0]
+    for q in range(1, 9):
+        whole = whole + raised[q]
+    weights = [r / whole for r in raised]
+    shift_y = (weights[6] + weights[7] + weights[8]) - (weights[0] + weights[1] + weights[2])
+    shift_x = (weights[2] + weights[5] + weights[8]) - (weights[0] + weights[3] + weights[6])
+    blend = weights[0] * scores[0]
+    for q in range(1, 9):
+        blend = blend + weights[q] * scores[q]
+    quality = 1.0 / (1.0 + jnp.exp(-ZSCALE * blend))
+    three = jnp.where(sub8 == 0, shift_y, jnp.where(sub8 == 1, shift_x, jnp.where(sub8 == 2, quality, 0.0)))
+    chosen = jnp.where(iota((SLOTS, 128), 0).astype(F32) == place_row, 1.0, 0.0).astype(BF16)
+    three = thirds_dot(three, chosen)[:, :PAIRS]
+    offs = offs_v[...].astype(F32) * (1.0 / FIXED)
+    move_y = offs[0:1] + three[0:1]
+    move_x = offs[1:2] + three[1:2]
+    quality = three[2:3]
+    measure_out[0] = move_y
+    measure_out[1] = move_x
+    measure_out[2] = quality
+
+    up = jnp.where(r8 < 4, jnp.broadcast_to(move_y, (8, PAIRS)), jnp.broadcast_to(move_x, (8, PAIRS)))
+    up = jnp.where(ours, up, 0.0)
+    down = jnp.where(ours & (r8 < 4), jnp.broadcast_to(quality, (8, PAIRS)), 0.0)
+    both = jnp.concatenate([up, down], axis=0)
+    mrow[pl.ds(0, 16), :] = thirds_dot(both, deal)
+
+    def mrow_copy(k):
+        return remote(mrow.at[pl.ds(0, 16)], mrow.at[pl.ds(16 * k, 16)], mrow_s.at[k], mrow_r.at[k], row_peer(k))
+
+    for k in range(1, ROW):
+        mrow_copy(k).start()
     for k in range(1, NZ):
         zsec_arrived(k)
 
@@ -325,83 +440,6 @@
             onehot[:, pl.ds(128 * c, 128)] = jnp.where(hit, 1.0, 0.0).astype(BF16)
             hit = jnp.broadcast_to(later[l][0][z : z + 1, :], (8, 128)) == down8
             member[pl.ds(8 * c, 8), :] = jnp.where(hit, 1.0, 0.0)
-
-    for c in range(CHUNKS):
-        (plus_copy if goes_plus(4, c) else minus_copy)(4, c).wait_recv()
-    serve(7)
-    for t in range(NZ):
-        for k in range(1, ROW):
-            x_arrived(t, k, block_of(t))
-
-    def score(d, carry):
-        pairs = [d * LINKS + l for l in range(LINKS)]
-        chip = [recv[jnp.clip(req[8, i], 0, NZ * ROW * 2 - 1)].astype(F32) for i in pairs]
-        lifted = []
-        for l, i in enumerate(pairs):
-            swapped = pltpu.roll(chip[l], CHIP, 1)
-            blocks = jnp.concatenate(
-                [
-                    jnp.where(left32, chip[l], 0.0).astype(BF16),
-                    jnp.where(left32, swapped, 0.0).astype(BF16),
-                    jnp.where(left32, 0.0, swapped).astype(BF16),
-                    jnp.where(left32, 0.0, chip[l]).astype(BF16),
-                ],
-                axis=0,
-            )
-            lifted.append(jnp.dot(lhs[i], blocks, preferred_element_type=F32).astype(BF16))
-        for l, i in enumerate(pairs):
-            up = lifted[l].astype(F32)
-            moved = mbuf[i].astype(F32)
-            for ky in range(3):
-                for kx in range(3):
-                    part = fold(up[32 * ky : 32 * ky + 32] * moved[:, 128 * kx : 128 * kx + 128])
-                    sums[pl.ds((3 * ky + kx) * PAIRS + i, 8, stride=ITEMS * PAIRS), :] = part
-            sums[pl.ds(9 * PAIRS + i, 8, stride=ITEMS * PAIRS), :] = fold(chip[l] * chip[l])
-            sums[pl.ds(10 * PAIRS + i, 8, stride=ITEMS * PAIRS), :] = bnorm[pl.ds(8 * d, 8), :]
-        return carry
-
-    lax.fori_loop(0, DATE_DEV, score, 0)
-
-    rows = []
-    for item in range(ITEMS):
-        part = sums[pl.ds(item * PAIRS, PAIRS), :]
-        for s in range(1, 8):
-            part = part + sums[pl.ds(s * ITEMS * PAIRS + item * PAIRS, PAIRS), :]
-        rows.append(jnp.sum(part.T, axis=0, keepdims=True))
-    size = CHIP / jnp.sqrt((rows[10] + EPS) * (rows[9] + EPS))
-    scores = [rows[q] * size for q in range(9)]
-    raised = [jnp.exp(ZSCALE * s) for s in scores]
-    whole = raised[0]
-    for q in range(1, 9):
-        whole = whole + raised[q]
-    weights = [r / whole for r in raised]
-    offs = offs_v[...].astype(F32) * (1.0 / FIXED)
-    move_y = offs[0:1] + ((weights[6] + weights[7] + weights[8]) - (weights[0] + weights[1] + weights[2]))
-    move_x = offs[1:2] + ((weights[2] + weights[5] + weights[8]) - (weights[0] + weights[3] + weights[6]))
-    blend = weights[0] * scores[0]
-    for q in range(1, 9):
-        blend = blend + weights[q] * scores[q]
-    quality = 1.0 / (1.0 + jnp.exp(-ZSCALE * blend))
-    measure_out[0] = move_y
-    measure_out[1] = move_x
-    measure_out[2] = quality
-
-    up = jnp.where(r8 < 4, jnp.broadcast_to(move_y, (8, PAIRS)), jnp.broadcast_to(move_x, (8, PAIRS)))
-    up = jnp.where(ours, up, 0.0)
-    down = jnp.where(ours & (r8 < 4), jnp.broadcast_to(quality, (8, PAIRS)), 0.0)
-    both = jnp.concatenate([up, down], axis=0)
-    first = both.astype(BF16)
-    rest = both - first.astype(F32)
-    second = rest.astype(BF16)
-    third = (rest - second.astype(F32)).astype(BF16)
-    dealt = jnp.dot(jnp.concatenate([first, second, third], axis=0), deal, preferred_element_type=F32)
-    mrow[pl.ds(0, 16), :] = dealt[0:16] + dealt[16:32] + dealt[32:48]
-
-    def mrow_copy(k):
-        return remote(mrow.at[pl.ds(0, 16)], mrow.at[pl.ds(16 * k, 16)], mrow_s.at[k], mrow_r.at[k], row_peer(k))
-
-    for k in range(1, ROW):
-        mrow_copy(k).start()
     for k in range(1, ROW):
         mrow_copy(k).wait_recv()
     total = mrow[pl.ds(0, 16), :]
@@ -523,9 +561,9 @@
                 plus_copy(s, c).wait_send()
             if goes_minus(s, c):
                 minus_copy(s, c).wait_send()
-    for t in range(NZ):
+    for g in range(len(GROUPS)):
         for k in range(1, ROW):
-            x_copy(t, k, block_of(t)).wait_send()
+            x_copy(g, k).wait_send()
     for n, side in ((0, 0), (0, 1), (0, 2), (0, 3), (1, 0), (1, 1)):
         halo_copy(n, side).wait_send()
 
@@ -536,7 +574,7 @@
     slot = pair_slot.reshape(1, PAIRS)
     offs = jnp.transpose(offset_fix.reshape(PAIRS, 2), (1, 0))
     vmem = pl.BlockSpec(memory_space=pltpu.VMEM)
-    anywhere = pl.BlockSpec(memory_space=pl.ANY)
+    anywhere = pl.BlockSpec(memory_space=pltpu.HBM)
     dma = pltpu.SemaphoreType.DMA
     measure, disp = pl.pallas_call(
         kernel,
@@ -554,9 +592,9 @@
             pltpu.VMEM((2, PAIRS), jnp.int32),
             pltpu.VMEM((DATE_DEV * 32 + 32, 128), F32),
             *[pltpu.VMEM((DATE_DEV, 32, 128), BF16)] * NZ,
-            pltpu.VMEM((NZ * ROW * 2, 32, 128), BF16),
-            pltpu.VMEM((NZ * ROW * 2, 32, 128), BF16),
-            pltpu.VMEM((DATE_DEV * 8, 128), F32),
+            pltpu.VMEM((ROW, NZ, 2, 32, 128), BF16),
+            pltpu.VMEM((NZ, ROW, 2, 32, 128), BF16),
+            pltpu.VMEM((DATE_DEV, 8, 128), F32),
             pltpu.VMEM((ROW * 16 + 8, 128), F32),
             pltpu.VMEM((NZ * 8 + 8, 128), F32),
             pltpu.VMEM((16, 128), jnp.int32),
@@ -565,7 +603,7 @@
             pltpu.VMEM((PAIRS, 96, 128), BF16),
             pltpu.VMEM((128, LINKS * NZ * 128), BF16),
             pltpu.VMEM((LINKS * NZ * 8, 128), F32),
-            pltpu.VMEM((9 * ITEMS * PAIRS, 128), F32),
+            pltpu.VMEM((SLOTS, 128), F32),
             pltpu.VMEM((ROW * 16, 128), F32),
             pltpu.VMEM((NZ * 16 + 16, 128), F32),
             pltpu.VMEM((48, LINKS * NZ * 128), BF16),
@@ -581,8 +619,8 @@
             dma((4, CHUNKS)),
             dma((4, CHUNKS)),
             dma((4, CHUNKS)),
-            dma((NZ, ROW)),
-            dma((NZ, ROW)),
+            dma((len(GROUPS), ROW)),
+            dma((len(GROUPS), ROW)),
             dma((ROW,)),
             dma((ROW,)),
             dma((NZ,)),

time: 60.9 us -> 56.9 us (0.934)
  Pallas kernels: 57.2 us -> 53.2 us
    pallas_call x1, Pallas kernels: 57.2 us -> 53.2 us  [per_device(): pl.pallas_call(kernel, out_shape=(jax.ShapeDtypeStruct((3, 1, PAIRS), F32...]
where the time goes in v3:
time: 56.9 us; the launch traced here: 56.6 us
  Pallas kernels  53.2 us (93%)
  local copies, waits for them, and re-layouts  2.7 us (5%)
  between operations  0.67 us (1%)
    pallas_call x1, Pallas kernels, per_device(): pl.pallas_call(kernel, out_shape=(jax.ShapeDtypeStruct((3, 1, PAIRS), F32...  53.2 us
    unnamed x10, local copies, waits for them, and re-layouts  2.7 us

profile of v3, /device:TPU:1, one launch (start us, length us, event | category | flops | bytes accessed | tf_op | source)
XLA Modules:
  0.0 56.6 jit_solution(1200764285477343641)
XLA Ops:
  0.6 0.0 copy-start.3
  0.6 0.0 copy-start.1
  0.7 0.0 copy-start.2
  0.7 0.6 %copy-done.3 = s32[64]{0:T(128)S(1)} copy-done((s32[64]{0:T(128)S(1)}, s32[64]{0:T(128)}, u32[]{:S(2)}) %copy-start.3) | copy-done | bytes 280
  1.3 0.0 copy-done.1
  1.3 0.0 copy-done.2
  1.3 0.0 copy-start
  1.3 0.9 %copy-done = bf16[16,1,4096]{2,0,1:T(8,128)(2,1)S(1)} copy-done((bf16[16,1,4096]{2,0,1:T(8,128)(2,1)S(1)}, bf16[16,1,4096]{2,0,1:T(8,128)(2,1)}, u32[]{:S(2)}) %copy-start) | copy-done | bytes 131096
  2.2 53.2 %offset_network.1 = (f32[3,1,64]{2,1,0:T(1,128)S(1)}, f32[2,1,16]{2,1,0:T(1,128)S(1)}) custom-call(bf16[16,4096]{1,0:T(8,128)(2,1)S(1)} %bitcast.10, s32[1,64]{1,0:T(1,128)S(1)} %bitcast.14, s32[1,64]{1,0:T(1,128)S(1)} %bitcast.15, s32[2,64]{1,0:T(2,128)S(1)} %bitcast.12), custom_call_target="tpu_custom_call" | custom-call | tf_op jit(solution)/shard_map/offset_network/pallas_call | solution.py:579
  55.5 0.6 copy.9
  56.0 0.6 copy.10
Async XLA Ops:
  0.6 0.7 %copy-start.3 = (s32[64]{0:T(128)S(1)}, s32[64]{0:T(128)}, u32[]{:S(2)}) copy-start(s32[64]{0:T(128)} %param.6) | copy-start | bytes 772
  0.6 0.7 %copy-start.1 = (s32[64,1,2]{0,2,1:T(2,128)S(1)}, s32[64,1,2]{0,2,1:T(2,128)}, u32[]{:S(2)}) copy-start(s32[64,1,2]{0,2,1:T(2,128)} %param.7) | copy-start | bytes 1540
  0.7 0.7 %copy-start.2 = (s32[64,1]{0,1:T(1,128)S(1)}, s32[64,1]{0,1:T(1,128)}, u32[]{:S(2)}) copy-start(s32[64,1]{0,1:T(1,128)} %param.5) | copy-start | bytes 772
  1.3 0.9 %copy-start = (bf16[16,1,4096]{2,0,1:T(8,128)(2,1)S(1)}, bf16[16,1,4096]{2,0,1:T(8,128)(2,1)}, u32[]{:S(2)}) copy-start(bf16[16,1,4096]{2,0,1:T(8,128)(2,1)} %param.4) | copy-start | bytes 393220

commit v4 on v3

--- a/solution.py
+++ b/solution.py
@@ -8,6 +8,7 @@
 CHIP = 64
 LINKS = 4
 ROW = 8
+FAR_FIRST = (4, 3, 5, 2, 6, 1, 7)
 NZ = 8
 DATE_DEV = 16
 PAIRS = 64
@@ -19,10 +20,10 @@
 LAMBDA = 2.0
 MUS = (4.0, 2.0, 1.0)
 FIXED = 32.0
-ITEMS = 11
+ITEMS = 10
 F32 = jnp.float32
 BF16 = jnp.bfloat16
-PRE = (7, 1, 2, 2, 4)
+PRE = (9, 2, 2, 3, 0)
 SLOTS = 128
 GROUPS = ((0,), (1, 2), (3, 4), (5, 6), (7,))
 
@@ -219,7 +220,7 @@
         plus_copy(1, c).start()
         minus_copy(1, c).start()
         if c == 0:
-            for k in range(1, ROW):
+            for k in FAR_FIRST:
                 row_copy(k).start()
 
     lane64 = iota((CHIP, 128), 1)
@@ -315,20 +316,8 @@
             if k:
                 x_copy(g, k).start()
 
-    serve(0)
-    serve(1)
-    for k in range(1, NZ):
-        zsec_copy(k).start()
-    prepare_part(1)
-    for s in (2, 3):
-        forward(s, range(CHUNKS))
-        serve(s)
-        prepare_part(s)
-    for c in range(CHUNKS):
-        (plus_copy if goes_plus(4, c) else minus_copy)(4, c).wait_recv()
-    serve(4)
-    prepare_part(4)
-
+    on_left = jnp.where(left32, 1.0, 0.0).astype(BF16)
+    on_right = jnp.where(left32, 0.0, 1.0).astype(BF16)
     sub8 = iota((8, 128), 0)
     lane8 = iota((8, 128), 1)
 
@@ -350,15 +339,10 @@
         chip = [recv[t, part * 4 + j // 2, j % 2].astype(F32) for j in range(8)]
         lifted = []
         for j in range(8):
-            swapped = pltpu.roll(chip[j], CHIP, 1)
+            swapped = pltpu.roll(chip[j], CHIP, 1).astype(BF16)
+            straight = chip[j].astype(BF16)
             blocks = jnp.concatenate(
-                [
-                    jnp.where(left32, chip[j], 0.0).astype(BF16),
-                    jnp.where(left32, swapped, 0.0).astype(BF16),
-                    jnp.where(left32, 0.0, swapped).astype(BF16),
-                    jnp.where(left32, 0.0, chip[j]).astype(BF16),
-                ],
-                axis=0,
+                [straight * on_left, swapped * on_left, swapped * on_right, straight * on_right], axis=0
             )
             lifted.append(jnp.dot(lhs[pairs[j]], blocks, preferred_element_type=F32).astype(BF16))
         items = [[] for _ in range(ITEMS)]
@@ -369,25 +353,42 @@
                 for kx in range(3):
                     items[3 * ky + kx].append(fold(up[32 * ky : 32 * ky + 32] * moved[:, 128 * kx : 128 * kx + 128]))
             items[9].append(fold(chip[j] * chip[j]))
-            items[10].append(bnorm[lax.div(pairs[j], LINKS)])
         table = jnp.zeros((8, 128), F32)
         for item in range(ITEMS):
             table = jnp.where(lane8 == item, jnp.sum(fold8(items[item]), axis=1, keepdims=True), table)
         sums[pl.ds(pl.multiple_of(t * 2 * ROW + part * 8, 8), 8), :] = table
 
-    for g in range(len(GROUPS)):
+    def score_group(g):
         for k in range(1, ROW):
             x_arrived(g, k)
-        first, count = GROUPS[g][0], len(GROUPS[g])
-
-        def score_step(n, carry, first=first):
-            score(first + lax.div(n, 2), lax.rem(n, 2))
-            return carry
-
-        lax.fori_loop(0, 2 * count, score_step, 0)
-
-    turned = sums[...].T
-    rows = [turned[item : item + 1, :] for item in range(ITEMS)]
+        for t in GROUPS[g]:
+            score(t, 0)
+            score(t, 1)
+
+    serve(0)
+    serve(1)
+    prepare_part(1)
+    for s in (2, 3):
+        forward(s, range(CHUNKS))
+        serve(s)
+        prepare_part(s)
+    for c in range(CHUNKS):
+        (plus_copy if goes_plus(4, c) else minus_copy)(4, c).wait_recv()
+    serve(4)
+    for k in FAR_FIRST:
+        zsec_copy(k).start()
+    prepare_part(4)
+
+    for g in range(len(GROUPS)):
+        score_group(g)
+
+    chosen = jnp.where(iota((SLOTS, 128), 0).astype(F32) == place_row, 1.0, 0.0).astype(BF16)
+    rows = thirds_dot(sums[...].T[:16], chosen)[:, :PAIRS]
+    rows = [rows[item : item + 1, :] for item in range(ITEMS)]
+    norms = jnp.concatenate([fold8([bnorm[8 * h + j] for j in range(8)]) for h in (0, 1)], axis=0)
+    norms = jnp.sum(norms, axis=1, keepdims=True)
+    leads = iota((DATE_DEV, PAIRS), 0) == iota((DATE_DEV, PAIRS), 1) // LINKS
+    rows.append(jnp.sum(jnp.where(leads, norms, 0.0), axis=0, keepdims=True))
     size = CHIP / jnp.sqrt((rows[10] + EPS) * (rows[9] + EPS))
     scores = [rows[q] * size for q in range(9)]
     raised = [jnp.exp(ZSCALE * s) for s in scores]
@@ -401,13 +402,9 @@
     for q in range(1, 9):
         blend = blend + weights[q] * scores[q]
     quality = 1.0 / (1.0 + jnp.exp(-ZSCALE * blend))
-    three = jnp.where(sub8 == 0, shift_y, jnp.where(sub8 == 1, shift_x, jnp.where(sub8 == 2, quality, 0.0)))
-    chosen = jnp.where(iota((SLOTS, 128), 0).astype(F32) == place_row, 1.0, 0.0).astype(BF16)
-    three = thirds_dot(three, chosen)[:, :PAIRS]
     offs = offs_v[...].astype(F32) * (1.0 / FIXED)
-    move_y = offs[0:1] + three[0:1]
-    move_x = offs[1:2] + three[1:2]
-    quality = three[2:3]
+    move_y = offs[0:1] + shift_y
+    move_x = offs[1:2] + shift_x
     measure_out[0] = move_y
     measure_out[1] = move_x
     measure_out[2] = quality
@@ -421,7 +418,7 @@
     def mrow_copy(k):
         return remote(mrow.at[pl.ds(0, 16)], mrow.at[pl.ds(16 * k, 16)], mrow_s.at[k], mrow_r.at[k], row_peer(k))
 
-    for k in range(1, ROW):
+    for k in FAR_FIRST:
         mrow_copy(k).start()
     for k in range(1, NZ):
         zsec_arrived(k)
@@ -431,13 +428,14 @@
         dev = zsec[pl.ds(l, NZ, stride=8), :].astype(jnp.int32)
         pos = zsec[pl.ds(4 + l, NZ, stride=8), :].astype(jnp.int32)
         later.append((dev // ROW, (dev % ROW) * DATE_DEV + pos))
-    down128 = iota((128, 128), 0)
+    across = iota((128, 128), 1).astype(F32)
     down8 = iota((8, 128), 0)
     for l in range(LINKS):
+        columns = later[l][1].astype(F32).T
         for z in range(NZ):
             c = l * NZ + z
-            hit = jnp.broadcast_to(later[l][1][z : z + 1, :], (128, 128)) == down128
-            onehot[:, pl.ds(128 * c, 128)] = jnp.where(hit, 1.0, 0.0).astype(BF16)
+            hit = columns[:, z : z + 1] == across
+            onehot[pl.ds(128 * c, 128), :] = jnp.where(hit, 1.0, 0.0).astype(BF16)
             hit = jnp.broadcast_to(later[l][0][z : z + 1, :], (8, 128)) == down8
             member[pl.ds(8 * c, 8), :] = jnp.where(hit, 1.0, 0.0)
     for k in range(1, ROW):
@@ -455,7 +453,7 @@
         theirs = mall.at[pl.ds(16 * lax.rem(mz - k + NZ, NZ), 16)]
         remote(theirs, theirs, mall_s.at[k], mall_r.at[k], z_peer(k)).wait_recv()
 
-    for k in range(1, NZ):
+    for k in FAR_FIRST:
         mall_copy(k).start()
     for k in range(1, NZ):
         mall_arrived(k)
@@ -511,7 +509,7 @@
                 low = (tall - high.astype(F32)).astype(BF16)
                 spread[:, pl.ds(128 * c, 128)] = jnp.concatenate([high, low], axis=0)
         sent = lax.dot_general(
-            spread[...], onehot[...], (((1,), (1,)), ((), ())), preferred_element_type=F32
+            spread[...], onehot[...], (((1,), (0,)), ((), ())), preferred_element_type=F32
         )
         sent = sent[0:24] + sent[24:48]
         numer = [numer[a] + sent[8 * a : 8 * a + 8] for a in range(2)]
@@ -520,7 +518,7 @@
             field = [numer[a] / (2.0 * LAMBDA + denom) for a in range(2)]
             for a in range(2):
                 fsend[pl.ds(8 * a, 8), :] = field[a]
-            for side in range(4):
+            for side in (2, 3, 0, 1):
                 halo_copy(0, side).start()
         elif n == 1:
             for a in range(2):
@@ -601,7 +599,7 @@
             pltpu.SMEM((16, 128), jnp.int32),
             pltpu.VMEM((PAIRS, 32, 384), BF16),
             pltpu.VMEM((PAIRS, 96, 128), BF16),
-            pltpu.VMEM((128, LINKS * NZ * 128), BF16),
+            pltpu.VMEM((LINKS * NZ * 128, 128), BF16),
             pltpu.VMEM((LINKS * NZ * 8, 128), F32),
             pltpu.VMEM((SLOTS, 128), F32),
             pltpu.VMEM((ROW * 16, 128), F32),

time: 56.9 us -> 51.8 us (0.910)
  Pallas kernels: 53.2 us -> 48.3 us
    pallas_call x1, Pallas kernels: 53.2 us -> 48.3 us  [per_device(): pl.pallas_call(kernel, out_shape=(jax.ShapeDtypeStruct((3, 1, PAIRS), F32...]
where the time goes in v4:
time: 51.8 us; the launch traced here: 51.7 us
  Pallas kernels  48.3 us (93%)
  local copies, waits for them, and re-layouts  2.7 us (5%)
  between operations  0.67 us (1%)
    pallas_call x1, Pallas kernels, per_device(): pl.pallas_call(kernel, out_shape=(jax.ShapeDtypeStruct((3, 1, PAIRS), F32...  48.3 us
    unnamed x10, local copies, waits for them, and re-layouts  2.7 us

profile of v4, /device:TPU:1, one launch (start us, length us, event | category | flops | bytes accessed | tf_op | source)
XLA Modules:
  0.0 51.7 jit_solution(15157010177613039582)
XLA Ops:
  0.6 0.0 copy-start.3
  0.6 0.0 copy-start.1
  0.7 0.0 copy-start.2
  0.7 0.6 %copy-done.3 = s32[64]{0:T(128)S(1)} copy-done((s32[64]{0:T(128)S(1)}, s32[64]{0:T(128)}, u32[]{:S(2)}) %copy-start.3) | copy-done | bytes 280
  1.3 0.0 copy-done.1
  1.3 0.0 copy-done.2
  1.3 0.0 copy-start
  1.3 0.9 %copy-done = bf16[16,1,4096]{2,0,1:T(8,128)(2,1)S(1)} copy-done((bf16[16,1,4096]{2,0,1:T(8,128)(2,1)S(1)}, bf16[16,1,4096]{2,0,1:T(8,128)(2,1)}, u32[]{:S(2)}) %copy-start) | copy-done | bytes 131096
  2.2 48.3 %offset_network.1 = (f32[3,1,64]{2,1,0:T(1,128)S(1)}, f32[2,1,16]{2,1,0:T(1,128)S(1)}) custom-call(bf16[16,4096]{1,0:T(8,128)(2,1)S(1)} %bitcast.10, s32[1,64]{1,0:T(1,128)S(1)} %bitcast.14, s32[1,64]{1,0:T(1,128)S(1)} %bitcast.15, s32[2,64]{1,0:T(2,128)S(1)} %bitcast.12), custom_call_target="tpu_custom_call" | custom-call | tf_op jit(solution)/shard_map/offset_network/pallas_call | solution.py:577
  50.5 0.6 %copy.9 = f32[2,16,1]{1,2,0:T(1,128)} copy(f32[2,16,1]{1,2,0:T(1,128)S(1)} %bitcast.13) | data formatting | bytes 256
  51.1 0.6 %copy.10 = f32[3,64,1]{1,2,0:T(1,128)} copy(f32[3,64,1]{1,2,0:T(1,128)S(1)} %bitcast.11) | data formatting | bytes 1536
Async XLA Ops:
  0.6 0.7 %copy-start.3 = (s32[64]{0:T(128)S(1)}, s32[64]{0:T(128)}, u32[]{:S(2)}) copy-start(s32[64]{0:T(128)} %param.6) | copy-start | bytes 772
  0.6 0.7 %copy-start.1 = (s32[64,1,2]{0,2,1:T(2,128)S(1)}, s32[64,1,2]{0,2,1:T(2,128)}, u32[]{:S(2)}) copy-start(s32[64,1,2]{0,2,1:T(2,128)} %param.7) | copy-start | bytes 1540
  0.7 0.7 %copy-start.2 = (s32[64,1]{0,1:T(1,128)S(1)}, s32[64,1]{0,1:T(1,128)}, u32[]{:S(2)}) copy-start(s32[64,1]{0,1:T(1,128)} %param.5) | copy-start | bytes 772
  1.3 0.9 %copy-start = (bf16[16,1,4096]{2,0,1:T(8,128)(2,1)S(1)}, bf16[16,1,4096]{2,0,1:T(8,128)(2,1)}, u32[]{:S(2)}) copy-start(bf16[16,1,4096]{2,0,1:T(8,128)(2,1)} %param.4) | copy-start | bytes 393220

commit v5 on v4

--- a/solution.py
+++ b/solution.py
@@ -630,7 +630,7 @@
             collective_id=0, has_side_effects=True, vmem_limit_bytes=40 * 1024 * 1024
         ),
         name="offset_network",
-    )(flat, target, slot, offs)
+    )(*[pltpu.with_memory_space_constraint(v, pltpu.HBM) for v in (flat, target, slot, offs)])
     return (jnp.transpose(disp, (0, 2, 1)), jnp.transpose(measure, (0, 2, 1)))
 
 

time: 51.8 us -> 50.2 us (0.969)
  local copies, waits for them, and re-layouts: 2.7 us -> 1.13 us
    unnamed x10 -> x2, local copies, waits for them, and re-layouts: 2.7 us -> 1.13 us
where the time goes in v5:
time: 50.2 us; the launch traced here: 50.1 us
  Pallas kernels  48.3 us (96%)
  local copies, waits for them, and re-layouts  1.13 us (2%)
  between operations  0.64 us (1%)
    pallas_call x1, Pallas kernels, per_device(): pl.pallas_call(kernel, out_shape=(jax.ShapeDtypeStruct((3, 1, PAIRS), F32...  48.3 us
    unnamed x2, local copies, waits for them, and re-layouts  1.13 us

profile of v5, /device:TPU:1, one launch (start us, length us, event | category | flops | bytes accessed | tf_op | source)
XLA Modules:
  0.0 50.1 jit_solution(9666671853033340504)
XLA Ops:
  0.6 48.3 %offset_network.1 = (f32[3,1,64]{2,1,0:T(1,128)S(1)}, f32[2,1,16]{2,1,0:T(1,128)S(1)}) custom-call(bf16[16,4096]{1,0:T(8,128)(2,1)} %bitcast.12, s32[1,64]{1,0:T(1,128)} %bitcast.14, s32[1,64]{1,0:T(1,128)} %bitcast.15, s32[2,64]{1,0:T(2,128)} %bitcast.13), custom_call_target="tpu_custom_call" | custom-call | tf_op jit(solution)/shard_map/offset_network/pallas_call | solution.py:577
  48.9 0.6 %copy.9 = f32[2,16,1]{1,2,0:T(1,128)} copy(f32[2,16,1]{1,2,0:T(1,128)S(1)} %bitcast.11) | data formatting | bytes 256
  49.5 0.6 %copy.10 = f32[3,64,1]{1,2,0:T(1,128)} copy(f32[3,64,1]{1,2,0:T(1,128)S(1)} %bitcast.10) | data formatting | bytes 1536

commit v6 on v5

--- a/solution.py
+++ b/solution.py
@@ -518,7 +518,7 @@
             field = [numer[a] / (2.0 * LAMBDA + denom) for a in range(2)]
             for a in range(2):
                 fsend[pl.ds(8 * a, 8), :] = field[a]
-            for side in (2, 3, 0, 1):
+            for side in range(4):
                 halo_copy(0, side).start()
         elif n == 1:
             for a in range(2):
@@ -526,12 +526,14 @@
             fsend[pl.ds(32, 8), :] = denom
             for side in (0, 1):
                 halo_copy(1, side).start()
-            for side in range(4):
+            for side in (0, 1):
                 halo_copy(0, side).wait_recv()
             near = [inside(-1, halo[0, pl.ds(8 * a, 8), :]) + inside(1, halo[1, pl.ds(8 * a, 8), :]) for a in range(2)]
             start = field
             field = settle(near, numer, denom)
         else:
+            for side in (2, 3):
+                halo_copy(0, side).wait_recv()
             for side in (0, 1):
                 halo_copy(1, side).wait_recv()
             beside = [0.0, 0.0]

time: 50.2 us -> 49.9 us (level)
  no operation moved by 1% of the time
where the time goes in v6:
time: 49.9 us; the launch traced here: 49.7 us
  Pallas kernels  48 us (96%)
  local copies, waits for them, and re-layouts  1.13 us (2%)
  between operations  0.64 us (1%)
    pallas_call x1, Pallas kernels, per_device(): pl.pallas_call(kernel, out_shape=(jax.ShapeDtypeStruct((3, 1, PAIRS), F32...  48 us
    unnamed x2, local copies, waits for them, and re-layouts  1.13 us

profile of v6, /device:TPU:1, one launch (start us, length us, event | category | flops | bytes accessed | tf_op | source)
XLA Modules:
  0.0 49.7 jit_solution(9243376165354472198)
XLA Ops:
  0.6 48.0 %offset_network.1 = (f32[3,1,64]{2,1,0:T(1,128)S(1)}, f32[2,1,16]{2,1,0:T(1,128)S(1)}) custom-call(bf16[16,4096]{1,0:T(8,128)(2,1)} %bitcast.12, s32[1,64]{1,0:T(1,128)} %bitcast.14, s32[1,64]{1,0:T(1,128)} %bitcast.15, s32[2,64]{1,0:T(2,128)} %bitcast.13), custom_call_target="tpu_custom_call" | custom-call | tf_op jit(solution)/shard_map/offset_network/pallas_call | solution.py:579
  48.6 0.6 %copy.9 = f32[2,16,1]{1,2,0:T(1,128)} copy(f32[2,16,1]{1,2,0:T(1,128)S(1)} %bitcast.11) | data formatting | bytes 256
  49.2 0.6 %copy.10 = f32[3,64,1]{1,2,0:T(1,128)} copy(f32[3,64,1]{1,2,0:T(1,128)S(1)} %bitcast.10) | data formatting | bytes 1536
